TPU v7x, 256 devices: a whole 4x4x8 slice. The times are simulated.
256 devices in a mesh: dp: 32 (over z, y), ctx: 8 (over x, core).
Axes of the slice: x: 4, y: 4, z: 8, core: 2. Of those that a mesh axis runs over, the one named last changes fastest.
Arguments:
- queries: bfloat16 [32768, 2048], P(('dp', 'ctx'))
- keys: bfloat16 [32768, 2048], P(('dp', 'ctx'))
- values: bfloat16 [32768, 2048], P(('dp', 'ctx')), may hold values from -6 to 6
- spans: int32 [32, 2], P('dp'), may hold values from 128 to 1023, as said below
- resid_in: bfloat16 [32768, 4096], P('dp'), may hold values from -2 to 2
- out_weight: bfloat16 [2048, 4096], P('ctx', 'dp'), may hold values from -0.375 to 0.375
- norm_gain: float32 [4096], replicated, may hold values from 0.1 to 1.9
- gate_weight: bfloat16 [4096, 5504], P('dp', 'ctx'), may hold values from -0.09375 to 0.09375
- up_weight: bfloat16 [4096, 5504], P('dp', 'ctx'), may hold values from -0.09375 to 0.09375
Outputs:
- resid_out: bfloat16 [32768, 4096], P(('dp', 'ctx'))
- hidden: bfloat16 [32768, 5504], P('dp', 'ctx')
Inputs may be any that keep to these rules, and one draw needn't show every extreme that they name: `spans`: in each slab, 128 <= prefix end <= 512 and prefix end < middle end <= 1023.
All inputs are finite; a program needn't handle non-finite values.
Results may differ from a plain program's by a relative error of at most 0.025.
Values may be sent and summed in bfloat16 or wider, within the bound.
A program may use at most 128 MiB of HBM per device.

v0:
```python
import jax
import jax.numpy as jnp
from jax import lax
from jax.sharding import PartitionSpec as P

HEAD_DIM = 128


def slab_ranks(prefix_end, middle_end, length):
    pos = lax.iota(jnp.int32, length)
    return jnp.where(
        pos < prefix_end,
        pos,
        jnp.where(
            pos >= middle_end,
            prefix_end + pos - middle_end,
            prefix_end + (length - middle_end) + (pos - prefix_end),
        ),
    )


def block_softmax(scores, allowed, vals):
    scores = jnp.where(allowed, scores, jnp.float32(-1e30))
    peak = jnp.max(scores, axis=-1, keepdims=True)
    expo = jnp.where(allowed, jnp.exp(scores - peak), jnp.float32(0.0))
    probs = (expo / jnp.sum(expo, axis=-1, keepdims=True)).astype(jnp.bfloat16)
    return jnp.einsum("hqk,khd->qhd", probs, vals, preferred_element_type=jnp.float32).astype(
        jnp.bfloat16
    )


def rms_normed(stream, norm_gain):
    scale = lax.rsqrt(jnp.mean(stream * stream, axis=-1, keepdims=True) + 1e-05)
    return (stream * scale * norm_gain).astype(jnp.bfloat16)


def body(queries, keys, values, spans, resid_in, out_weight, norm_gain, gate_weight, up_weight):
    tok_rows = queries.shape[0]
    q_heads, k_heads, v_heads = (
        lax.all_to_all(queries, "ctx", split_axis=1, concat_axis=0, tiled=True),
        lax.all_to_all(keys, "ctx", split_axis=1, concat_axis=0, tiled=True),
        lax.all_to_all(values, "ctx", split_axis=1, concat_axis=0, tiled=True),
    )
    length = q_heads.shape[0]
    local_heads = q_heads.shape[1] // HEAD_DIM
    q_three = q_heads.reshape(length, local_heads, HEAD_DIM)
    k_three = k_heads.reshape(length, local_heads, HEAD_DIM)
    v_three = v_heads.reshape(length, local_heads, HEAD_DIM)
    scaling = 1.0 / jnp.sqrt(jnp.float32(HEAD_DIM))
    rank = slab_ranks(spans[0, 0], spans[0, 1], length)
    block = min(512, length)
    pieces = []
    for start in range(0, length, block):
        stop = start + block
        scores = (
            jnp.einsum(
                "qhd,khd->hqk", q_three[start:stop], k_three, preferred_element_type=jnp.float32
            )
            * scaling
        )
        allowed = (rank[start:stop, None] >= rank[None, :])[None]
        pieces.append(block_softmax(scores, allowed, v_three))
    context = jnp.concatenate(pieces, axis=0)
    context = context.reshape(length, local_heads * HEAD_DIM)
    partial_out = jnp.dot(
        context,
        lax.all_gather(out_weight, "dp", axis=1, tiled=True),
        preferred_element_type=jnp.float32,
    )
    row_start = lax.axis_index("ctx") * tok_rows
    attn_total = lax.psum(partial_out.astype(jnp.bfloat16), "ctx").astype(jnp.float32)
    stream_all = resid_in.astype(jnp.float32) + attn_total
    normed = rms_normed(stream_all, norm_gain)
    resid_out = lax.dynamic_slice_in_dim(stream_all, row_start, tok_rows, 0).astype(jnp.bfloat16)
    gate = jnp.dot(
        normed,
        lax.all_gather(gate_weight, "dp", axis=0, tiled=True),
        preferred_element_type=jnp.float32,
    )
    up = jnp.dot(
        normed,
        lax.all_gather(up_weight, "dp", axis=0, tiled=True),
        preferred_element_type=jnp.float32,
    )
    hidden = (jax.nn.silu(gate) * up).astype(jnp.bfloat16)
    return (resid_out, hidden)


def solution(mesh):
    return jax.shard_map(
        body,
        mesh=mesh,
        in_specs=(
            P(("dp", "ctx"), None),
            P(("dp", "ctx"), None),
            P(("dp", "ctx"), None),
            P("dp", None),
            P("dp", None),
            P("ctx", "dp"),
            P(),
            P("dp", "ctx"),
            P("dp", "ctx"),
        ),
        out_specs=(P(("dp", "ctx"), None), P("dp", "ctx")),
        check_vma=False,
    )
```

profile of v0, /device:TPU:9, one launch (start us, length us, event | category | flops | bytes accessed | tf_op | source)
XLA Modules:
  0.0 403.7 jit_solution(5401266908982216098)
XLA Ops:
  7.2 0.0 copy-start
  7.2 0.0 copy-start.2
  7.2 0.0 all-gather.4.cloned.1.call-start
  7.2 0.7 all-gather.4.cloned.1.call-update
  7.9 2.0 copy.22
  10.0 5.0 %all-to-all-start.1 = ((bf16[128,8,256]{0,2,1:T(8,128)(2,1)}), bf16[128,8,256]{0,2,1:T(8,128)(2,1)S(1)}, u32[]{:S(2)}, u32[]{:S(2)}) async-start(bf16[128,8,256]{0,2,1:T(8,128)(2,1)} %bitcast.3), calls=%async_computation.1 | async-start | bytes 1048576 | tf_op jit(solution)/shard_map/all_to_all | solution.py:41
  14.9 1.9 copy.63
  16.8 7.6 %all-to-all-done.1 = bf16[128,8,256]{0,2,1:T(8,128)(2,1)S(1)} async-done(((bf16[128,8,256]{0,2,1:T(8,128)(2,1)}), bf16[128,8,256]{0,2,1:T(8,128)(2,1)S(1)}, u32[]{:S(2)}, u32[]{:S(2)}) %all-to-all-start.1) | async-done | bytes 524320 | tf_op jit(solution)/shard_map/all_to_all | solution.py:41
  24.4 4.3 %all-to-all-start = ((bf16[128,8,256]{2,0,1:T(8,128)(2,1)}), bf16[128,8,256]{2,0,1:T(8,128)(2,1)S(1)}, u32[]{:S(2)}, u32[]{:S(2)}) async-start(bf16[128,8,256]{2,0,1:T(8,128)(2,1)} %bitcast.29), calls=%async_computation | async-start | bytes 1048576 | tf_op jit(solution)/shard_map/all_to_all | solution.py:40
  28.7 0.0 copy-done
  28.7 1.0 copy.26
  29.7 0.0 copy-done.2
  29.7 0.6 fusion.41
  31.6 1.3 select_select_fusion
  32.9 5.3 %all-to-all-done = bf16[128,8,256]{2,0,1:T(8,128)(2,1)S(1)} async-done(((bf16[128,8,256]{2,0,1:T(8,128)(2,1)}), bf16[128,8,256]{2,0,1:T(8,128)(2,1)S(1)}, u32[]{:S(2)}, u32[]{:S(2)}) %all-to-all-start) | async-done | bytes 524320 | tf_op jit(solution)/shard_map/all_to_all | solution.py:40
  38.2 4.3 %all-to-all-start.2 = ((bf16[128,8,256]{0,2,1:T(8,128)(2,1)}), bf16[128,8,256]{0,2,1:T(8,128)(2,1)S(1)}, u32[]{:S(2)}, u32[]{:S(2)}) async-start(bf16[128,8,256]{0,2,1:T(8,128)(2,1)} %bitcast.5), calls=%async_computation.2 | async-start | bytes 1048576 | tf_op jit(solution)/shard_map/all_to_all | solution.py:42
  42.5 0.0 all-reduce.2.cloned.1.call-start
  42.5 0.7 broadcast_compare_fusion.1
  43.1 0.3 copy.23
  43.5 1.0 reshape.108
  44.5 0.1 slice.28
  44.6 7.4 %all-to-all-done.2 = bf16[128,8,256]{0,2,1:T(8,128)(2,1)S(1)} async-done(((bf16[128,8,256]{0,2,1:T(8,128)(2,1)}), bf16[128,8,256]{0,2,1:T(8,128)(2,1)S(1)}, u32[]{:S(2)}, u32[]{:S(2)}) %all-to-all-start.2) | async-done | bytes 524320 | tf_op jit(solution)/shard_map/all_to_all | solution.py:42
  52.0 0.3 copy.27
  52.3 0.2 reshape.109
  52.5 0.1 slice.31
  52.6 0.0 copy-done.1
  52.6 4.0 fusion.47
  56.6 4.0 fusion.42
  60.7 3.1 fusion.14
  63.8 0.4 copy-done.4
  64.1 0.8 fusion.15
  65.0 0.2 copy.32
  65.2 20.2 %all-gather.4.cloned.1.call-done = bf16[256,4096]{1,0:T(8,128)(2,1)} async-done(((bf16[256,128]{1,0:T(8,128)(2,1)}), bf16[256,4096]{1,0:T(8,128)(2,1)}) %all-gather.4.cloned.1.call-update) | async-done | bytes 2097168 | tf_op jit(solution)/shard_map/all_gather | solution.py:67
  85.4 7.2 %convolution_convert_fusion = bf16[1024,4096]{1,0:T(8,128)(2,1)} fusion(bf16[1024,256]{0,1:T(8,128)(2,1)S(1)} %bitcast.33, bf16[256,4096]{1,0:T(8,128)(2,1)} %all-gather.4.cloned.1.call-done), kind=kOutput, calls=%fused_computation.5 | convolution fusion | flops 2151677952 | bytes 11010048 | tf_op jit(solution)/shard_map/dot_general | solution.py:65
  92.6 0.0 all-reduce.2.cloned.1.call-update
  92.6 0.0 all-gather.6.cloned.1.call-start
  92.7 0.7 all-gather.6.cloned.1.call-update
  93.3 0.2 all-gather.8.cloned.1.call-start
  93.6 0.3 all-gather.8.cloned.1.call-update
  93.9 109.7 %all-reduce.2.cloned.1.call-done = bf16[1024,4096]{1,0:T(8,128)(2,1)} async-done(((bf16[1024,4096]{1,0:T(8,128)(2,1)}), bf16[1024,4096]{1,0:T(8,128)(2,1)}) %all-reduce.2.cloned.1.call-update) | async-done | bytes 8388624 | tf_op jit(solution)/shard_map/psum | solution.py:71
  203.7 8.5 %multiply_reduce_fusion = f32[1024]{0:T(1024)S(1)} fusion(bf16[1024,4096]{1,0:T(8,128)(2,1)} %all-reduce.2.cloned.1.call-done, bf16[1024,4096]{1,0:T(8,128)(2,1)} %param.13), kind=kLoop, calls=%fused_computation.3 | loop fusion | flops 20970496 | bytes 16781312 | tf_op jit(solution)/shard_map/reduce_sum | solution.py:33
  212.2 0.0 copy-start.3
  212.2 7.5 %convert_add_fusion = bf16[1024,4096]{1,0:T(8,128)(2,1)S(1)} fusion(bf16[1024,4096]{1,0:T(8,128)(2,1)} %all-reduce.2.cloned.1.call-done, bf16[1024,4096]{1,0:T(8,128)(2,1)} %param.13), kind=kLoop, calls=%fused_computation.4 | loop fusion | flops 16777216 | bytes 25165824 | tf_op jit(solution)/shard_map/add | solution.py:72
  219.8 1.1 dynamic-slice_convert_fusion
  220.8 72.3 %all-gather.6.cloned.1.call-done = bf16[4096,688]{0,1:T(8,128)(2,1)} async-done(((bf16[128,688]{0,1:T(8,128)(2,1)}), bf16[4096,688]{0,1:T(8,128)(2,1)}) %all-gather.6.cloned.1.call-update) | async-done | bytes 5636112 | tf_op jit(solution)/shard_map/all_gather | solution.py:77
  293.1 11.8 %fusion.38 = f32[1024,688]{0,1:T(8,128)S(1)} fusion(bf16[4096,688]{0,1:T(8,128)(2,1)} %all-gather.6.cloned.1.call-done, f32[4096]{0:T(1024)S(1)} %copy-done.3, f32[1024]{0:T(1024)S(1)} %add_rsqrt_fusion, bf16[1024,4096]{1,0:T(8,128)(2,1)} %all-reduce.2.cloned.1.call-done, bf16[1024,4096]{1,0:T(8,128)(2,1)} %param.13), kind=kOutput, calls=%fused_computation.48 | convolution fusion | flops 5796528128 | bytes 25251840 | tf_op jit(solution)/shard_map/dot_general | solution.py:75
  304.9 79.4 %all-gather.8.cloned.1.call-done = bf16[4096,688]{0,1:T(8,128)(2,1)} async-done(((bf16[128,688]{0,1:T(8,128)(2,1)}), bf16[4096,688]{0,1:T(8,128)(2,1)}) %all-gather.8.cloned.1.call-update) | async-done | bytes 5636112 | tf_op jit(solution)/shard_map/all_gather | solution.py:82
  384.3 12.9 %multiply_convert_fusion.1 = bf16[1024,688]{0,1:T(8,128)(2,1)} fusion(f32[1024,688]{0,1:T(8,128)S(1)} %fusion.38, bf16[4096,688]{0,1:T(8,128)(2,1)} %all-gather.8.cloned.1.call-done, f32[4096]{0:T(1024)S(1)} %copy-done.3, f32[1024]{0:T(1024)S(1)} %add_rsqrt_fusion, bf16[1024,4096]{1,0:T(8,128)(2,1)} %all-reduce.2.cloned.1.call-done, ...), kind=kOutput, calls=%fused_computation.14 | convolution fusion | flops 5800755200 | bytes 26660864 | tf_op jit(solution)/shard_map/dot_general | solution.py:80
  (7 shorter events, 0.1 us)
Async XLA Ops:
  7.2 21.5 %copy-start = (bf16[128,2048]{1,0:T(8,128)(2,1)S(1)}, bf16[128,2048]{1,0:T(8,128)(2,1)}, u32[]{:S(2)}) copy-start(bf16[128,2048]{1,0:T(8,128)(2,1)} %param.11) | copy-start | bytes 1572868
  7.2 22.5 %copy-start.2 = (s32[1,2]{1,0:T(1,128)S(1)}, s32[1,2]{1,0:T(1,128)}, u32[]{:S(2)}) copy-start(s32[1,2]{1,0:T(1,128)} %param.12) | copy-start | bytes 28
  7.2 78.2 %all-gather.4.cloned.1.call-start = ((), (), s32[]{:S(2)}) async-start(), calls=%async_computation.3 | async-start | bytes 2162688 | tf_op jit(solution)/shard_map/all_gather | solution.py:67
  10.0 14.5 %all-to-all-start.1 = ((bf16[128,8,256]{0,2,1:T(8,128)(2,1)}), bf16[128,8,256]{0,2,1:T(8,128)(2,1)S(1)}, u32[]{:S(2)}, u32[]{:S(2)}) async-start(bf16[128,8,256]{0,2,1:T(8,128)(2,1)} %bitcast.3), calls=%async_computation.1 | async-start | bytes 1048576 | tf_op jit(solution)/shard_map/all_to_all | solution.py:41
  24.4 13.8 %all-to-all-start = ((bf16[128,8,256]{2,0,1:T(8,128)(2,1)}), bf16[128,8,256]{2,0,1:T(8,128)(2,1)S(1)}, u32[]{:S(2)}, u32[]{:S(2)}) async-start(bf16[128,8,256]{2,0,1:T(8,128)(2,1)} %bitcast.29), calls=%async_computation | async-start | bytes 1048576 | tf_op jit(solution)/shard_map/all_to_all | solution.py:40
  38.2 13.8 %all-to-all-start.2 = ((bf16[128,8,256]{0,2,1:T(8,128)(2,1)}), bf16[128,8,256]{0,2,1:T(8,128)(2,1)S(1)}, u32[]{:S(2)}, u32[]{:S(2)}) async-start(bf16[128,8,256]{0,2,1:T(8,128)(2,1)} %bitcast.5), calls=%async_computation.2 | async-start | bytes 1048576 | tf_op jit(solution)/shard_map/all_to_all | solution.py:42
  42.5 161.2 %all-reduce.2.cloned.1.call-start = ((), (), s32[]{:S(2)}) async-start(), calls=%async_computation.4 | async-start | bytes 16777216 | tf_op jit(solution)/shard_map/psum | solution.py:71
  44.5 8.1 %copy-start.1 = (bf16[1024,2,128]{0,2,1:T(8,128)(2,1)S(1)}, bf16[1024,2,128]{0,2,1:T(8,128)(2,1)}, u32[]{:S(2)}) copy-start(bf16[1024,2,128]{0,2,1:T(8,128)(2,1)} %reshape.108) | copy-start | bytes 1572868
  60.7 3.5 copy-start.4
  92.6 200.5 %all-gather.6.cloned.1.call-start = ((), (), s32[]{:S(2)}) async-start(), calls=%async_computation.5 | async-start | bytes 5812224 | tf_op jit(solution)/shard_map/all_gather | solution.py:77
  93.3 290.9 %all-gather.8.cloned.1.call-start = ((), (), s32[]{:S(2)}) async-start(), calls=%async_computation.6 | async-start | bytes 5812224 | tf_op jit(solution)/shard_map/all_gather | solution.py:82
  212.2 80.9 %copy-start.3 = (f32[4096]{0:T(1024)S(1)}, f32[4096]{0:T(1024)}, u32[]{:S(2)}) copy-start(f32[4096]{0:T(1024)} %param.15) | copy-start | bytes 49156
Sparse Core Ops, SparseCore 0:
  10.5 74.8 all-gather.3
  92.7 110.8 all-reduce.1
  206.1 86.9 all-gather.5
  295.4 88.8 all-gather.7
where the time goes:
time: 408 us; the launch traced here: 404 us
  waiting for transfers between devices  304 us (75%)
  matrix products  43.8 us (11%)
  other arithmetic  18 us (4%)
  between operations  15.1 us (4%)
  starting transfers between devices  13.8 us (3%)
  local copies, waits for them, and re-layouts  9.3 us (2%)
    psum x1, waiting for transfers between devices, body(): lax.psum(partial_out.astype(jnp.bfloat16), 'ctx').astype(jnp.float32)  110 us
    all_gather x1, waiting for transfers between devices, body(): lax.all_gather(up_weight, 'dp', axis=0, tiled=True)  79.4 us
    all_gather x1, waiting for transfers between devices, body(): lax.all_gather(gate_weight, 'dp', axis=0, tiled=True)  72.3 us
    all_gather x1, waiting for transfers between devices, body(): lax.all_gather(out_weight, 'dp', axis=1, tiled=True)  20.2 us
    dot_general x1, matrix products, body(): jnp.dot(normed, lax.all_gather(up_weight, 'dp', axis=0, tiled=True), pref...  12.9 us
    dot_general x1, matrix products, body(): jnp.dot(normed, lax.all_gather(gate_weight, 'dp', axis=0, tiled=True), pr...  11.8 us
    reduce_sum x1, other arithmetic, rms_normed(): scale = lax.rsqrt(jnp.mean(stream * stream, axis=-1, keepdims=True) + 1e-05)  8.53 us
  transfers between devices with their start and end apart: 7, of which 7 were waited for; matrix products, arithmetic and copies ran while one was open for 13% of the time, Pallas kernels for 0%

commit v1 on v0

v1 whole, which is shorter than its diff:
```python
import functools
import math

import jax
import jax.numpy as jnp
from jax import lax
from jax.experimental import pallas as pl
from jax.experimental.pallas import tpu as pltpu
from jax.sharding import PartitionSpec as P

MESH = pl.DeviceIdType.MESH
Z, Y, X = 8, 4, 4
HD = 128
SEQ, D, FF = 1024, 4096, 688
N_BLOCKS = FF // 128
TAIL = FF - 128 * N_BLOCKS
WIDE = 256 * N_BLOCKS + 128
PART_COLS = {"A": (0, 512), "B": (512, WIDE - 512)}
EXP2_SCALE = math.log2(math.e) / math.sqrt(HD)
F32, BF16 = jnp.float32, jnp.bfloat16
N_SEMS = 256


def mult(value, of):
    return pl.multiple_of(value, of)


def kernel(
    q_in, k_in, v_in, spans, resid, wo_in, gain, gate_in, up_in,
    resid_out, hidden,
    qkv, ctx_own, ctx_all, res, stream, wo, w, hid, out_rows,
    send_sem, recv_sem, local_sem,
):
    cx, dp = lax.axis_index("ctx"), lax.axis_index("dp")
    x, c = cx // 2, cx % 2
    z, y = dp // Y, dp % Y

    def dev(dz=0, dy=0, dx=0, dc=0):
        zz, yy = (z + dz + Z) % Z, (y + dy + Y) % Y
        xx, cc = (x + dx + X) % X, (c + dc) % 2
        return (zz * Y + yy, xx * 2 + cc)

    recv_ids, sent, state = {}, [], {"send": 0, "local": 0}

    def recv_id(key):
        return recv_ids.setdefault(key, len(recv_ids))

    def send(src, dst, target, key, when=None):
        index = state["send"]
        state["send"] += 1
        copy = pltpu.make_async_remote_copy(
            src_ref=src, dst_ref=dst, send_sem=send_sem.at[index], recv_sem=recv_sem.at[recv_id(key)],
            device_id=target, device_id_type=MESH,
        )
        copy.start()
        if when is None:
            sent.append(copy)
        return copy

    def recv(dst, key):
        pltpu.make_async_remote_copy(
            src_ref=dst, dst_ref=dst, send_sem=send_sem.at[0], recv_sem=recv_sem.at[recv_id(key)],
            device_id=dev(0, 0, 0, 1), device_id_type=MESH,
        ).wait_recv()

    def local(src, dst):
        copy = pltpu.make_async_copy(src, dst, local_sem.at[state["local"]])
        state["local"] += 1
        copy.start()
        return copy

    barrier = pltpu.get_barrier_semaphore()
    peers = [(0, 0, dx, dc) for dx in range(X) for dc in range(2) if (dx, dc) != (0, 0)]
    peers += [(0, 1, 0, 0), (0, 2, 0, 0), (0, 3, 0, 0), (1, 0, 0, 0), (-1, 0, 0, 0)]
    for peer in peers:
        pl.semaphore_signal(barrier, inc=1, device_id=dev(*peer), device_id_type=MESH)
    pl.semaphore_wait(barrier, len(peers))

    mine = pl.ds(mult(cx * 128, 128), 128)
    shares = [(1, k_in), (2, v_in), (0, q_in)]
    order = [(dx, dc) for dx in (2, 1, 3, 0) for dc in range(2) if (dx, dc) != (0, 0)]
    for which, source in shares:
        for dx, dc in order:
            target = dev(0, 0, dx, dc)
            columns = pl.ds(mult(target[1] * 256, 256), 256)
            send(source.at[:, columns], qkv.at[which, mine], target, ("qkv", which, dx, dc))
    own_columns = pl.ds(mult(cx * 256, 256), 256)
    loads = [local(source.at[:, own_columns], qkv.at[which, mine]) for which, source in shares]
    res_loads = []
    for zz in range(Z):
        columns = pl.ds(mult(zz * 512 + x * 128, 128), 128)
        res_loads.append(local(resid.at[:, c, :, columns], res.at[:, :, pl.ds(zz * 128, 128)]))

    def wo_block(zz, cc, half=None):
        rows = pl.ds(mult(cc * 1024, 1024), 1024) if half is None else pl.ds(mult(cc * 1024 + half * 512, 512), 512)
        return wo.at[rows, pl.ds(mult(zz * 128, 128), 128)]

    def wo_rows(xx):
        return wo.at[pl.ds(mult(c * 1024 + xx * 256, 256), 256), pl.ds(mult(z * 128, 128), 128)]

    collector = x == y
    gather = {}
    wo_first = state["send"]
    state["send"] += 4
    for ahead in range(1, X):
        gather[ahead] = pltpu.make_async_remote_copy(
            src_ref=wo_in, dst_ref=wo_rows(x), send_sem=send_sem.at[wo_first],
            recv_sem=recv_sem.at[recv_id(("wo_x", ahead))], device_id=dev(0, 0, ahead, 0), device_id_type=MESH,
        )

        @pl.when((x + ahead) % X == y)
        def _(copy=gather[ahead]):
            copy.start()

    diagonal = lax.broadcasted_iota(jnp.int32, (128, 128), 0) == lax.broadcasted_iota(jnp.int32, (128, 128), 1)
    gain_row = gain[pl.ds(dp, 1), :]
    gain_column = jnp.sum(jnp.where(diagonal, gain_row, 0.0), axis=1, keepdims=True)

    def w_rows(zz, yy, half=None):
        start = (yy % Y) * 1024 + (zz % Z) * 128
        return pl.ds(mult(start, 128), 128) if half is None else pl.ds(mult(start + half * 64, 64), 64)

    own = w_rows(z, y)
    for block in range(N_BLOCKS):
        at = 256 * block
        w[own, at : at + 128] = (gate_in[:, 128 * block : 128 * block + 128].astype(F32) * gain_column).astype(BF16)
        w[own, at + 128 : at + 256] = (up_in[:, 128 * block : 128 * block + 128].astype(F32) * gain_column).astype(BF16)
    tails = jnp.concatenate(
        [gate_in[:, 128 * N_BLOCKS :].astype(F32), up_in[:, 128 * N_BLOCKS :].astype(F32), jnp.zeros((128, 128 - 2 * TAIL), F32)],
        axis=1,
    )
    w[own, 256 * N_BLOCKS :] = (tails * gain_column).astype(BF16)

    def w_block(part, dz, dy, half=None):
        first, count = PART_COLS[part]
        return w.at[w_rows(z + dz + Z, y + dy + Y, half), first : first + count]

    def z_send(part, dz, dy, d, key, half=None):
        ref = w_block(part, dz, dy, half)
        send(ref, ref, dev(d, 0, 0, 0), key)

    def y_send(part, dz, dy, d, key, half=None):
        ref = w_block(part, dz, dy, half)
        send(ref, ref, dev(0, d, 0, 0), key)

    def z_start(part, dy):
        for d in (1, -1):
            z_send(part, 0, dy, d, (part, "z", dy, d, 1))

    def z_wait(part, dy, hop):
        for d in (1, -1):
            half = None if hop < 4 else (0 if d == 1 else 1)
            recv(w_block(part, -d * hop, dy, half), (part, "z", dy, d, hop))

    def z_pass(part, dy, hop):
        for d in (1, -1):
            half = None if hop < 3 else (0 if d == 1 else 1)
            z_send(part, -d * hop, dy, d, (part, "z", dy, d, hop + 1), half)

    def z_event(part, dy, hop):
        z_wait(part, dy, hop)
        if hop < 4:
            z_pass(part, dy, hop)

    def y_start(part, dz):
        for d in (1, -1):
            y_send(part, dz, 0, d, (part, "y", dz, d, 1))

    def y_event(part, dz, hop):
        for d in (1, -1):
            half = None if hop < 2 else (0 if d == 1 else 1)
            recv(w_block(part, dz, -d * hop, half), (part, "y", dz, d, hop))
            if hop == 1:
                half = 0 if d == 1 else 1
                y_send(part, dz, -d, d, (part, "y", dz, d, 2), half)

    y_start("A", 0)
    z_start("B", 0)
    z_start("A", 0)
    y_start("B", 0)

    @pl.when(collector)
    def _():
        for ahead in range(1, X):
            recv(wo_rows((x - ahead + X) % X), ("wo_x", ahead))
        wo[pl.ds(mult(c * 1024 + x * 256, 256), 256), pl.ds(mult(z * 128, 128), 128)] = wo_in[...]

    spread = []
    for ahead in range(1, Y):
        spread.append(
            pltpu.make_async_remote_copy(
                src_ref=wo_block(z, c), dst_ref=wo_block(z, c), send_sem=send_sem.at[wo_first + ahead],
                recv_sem=recv_sem.at[recv_id("wo_y")], device_id=dev(0, ahead, 0, 0), device_id_type=MESH,
            )
        )

        @pl.when(collector)
        def _(copy=spread[-1]):
            copy.start()

    y_event("A", 0, 1)
    z_start("A", -1)

    @pl.when(jnp.logical_not(collector))
    def _():
        recv(wo_block(z, c), "wo_y")

    def wo_across(dz, half=None):
        ref = wo_block((z + dz + Z) % Z, c, half)
        send(ref, ref, dev(0, 0, 0, 1), ("wo_d", dz, half))

    def wo_event(hop):
        for d in (1, -1):
            half = None if hop < 4 else (0 if d == 1 else 1)
            ref = wo_block((z - d * hop + Z) % Z, c, half)
            recv(ref, ("wo_z", d, hop))
            if hop < 4:
                half_on = None if hop < 3 else (0 if d == 1 else 1)
                ref = wo_block((z - d * hop + Z) % Z, c, half_on)
                send(ref, ref, dev(d, 0, 0, 0), ("wo_z", d, hop + 1))
            wo_across(4 if hop == 4 else -d * hop, half)

    for d in (1, -1):
        ref = wo_block(z, c)
        send(ref, ref, dev(d, 0, 0, 0), ("wo_z", d, 1))
    wo_across(0)
    y_event("A", 0, 2)
    z_wait("B", 0, 1)
    y_start("B", 1)
    y_start("B", -1)
    wo_event(1)

    for copy in loads:
        copy.wait()
    for which, _ in shares:
        for dx, dc in order:
            rows = pl.ds(mult(dev(0, 0, -dx, dc)[1] * 128, 128), 128)
            recv(qkv.at[which, rows], ("qkv", which, dx, dc))

    prefix_end, middle_end = spans[0, 0], spans[0, 1]

    def ranks(pos):
        late = prefix_end + (SEQ - middle_end) + (pos - prefix_end)
        return jnp.where(pos < prefix_end, pos, jnp.where(pos >= middle_end, prefix_end + pos - middle_end, late))

    key_rank = ranks(lax.broadcasted_iota(jnp.int32, (1, SEQ), 1))

    def ctx_spot(k, cc, xx, half=None):
        rows = pl.ds(128 * k, 128) if half is None else pl.ds(128 * k + 64 * half, 64)
        return ctx_all.at[rows, pl.ds(mult(cc * 1024 + xx * 256, 256), 256)]

    def attend(k, rel):
        row = mult((2 * k + (c + rel) % 2) * 128, 128)
        rows = pl.ds(row, 128)
        query_rank = ranks(row + lax.broadcasted_iota(jnp.int32, (128, 1), 0))
        allowed = query_rank >= key_rank
        for head in range(2):
            cols = slice(head * HD, head * HD + HD)
            scores = lax.dot_general(
                qkv[0, rows, cols], qkv[1, :, cols], (((1,), (1,)), ((), ())), preferred_element_type=F32
            )
            scores = jnp.where(allowed, scores, -jnp.inf)
            peak = jnp.max(scores, axis=1, keepdims=True)
            expo = jnp.exp2((scores - peak) * EXP2_SCALE)
            total = jnp.sum(expo, axis=1, keepdims=True)
            mixed = jnp.dot(expo.astype(BF16), qkv[2, :, cols], preferred_element_type=F32)
            mixed = (mixed / total).astype(BF16)
            ctx_own[rows, cols] = mixed
            if rel == 0:
                ctx_all[128 * k : 128 * k + 128, pl.ds(mult(c * 1024 + x * 256 + head * HD, 128), HD)] = mixed
        for d in (1, -1):
            send(ctx_own.at[rows], ctx_spot(k, c, x), dev(0, 0, d, rel), ("ctx", k, rel, d, 1))
        if rel == 1:
            send(ctx_own.at[rows], ctx_spot(k, c, x), dev(0, 0, 0, 1), ("ctx_d", k))

    def ctx_pass(k):
        for rel in range(2):
            cc = (c + rel) % 2
            for d in (1, -1):
                recv(ctx_spot(k, cc, (x - d + X) % X), ("ctx", k, rel, d, 1))
                ref = ctx_spot(k, cc, (x - d + X) % X, 0 if d == 1 else 1)
                send(ref, ref, dev(0, 0, d, 0), ("ctx", k, rel, d, 2))

    def ctx_end(k):
        recv(ctx_spot(k, (c + 1) % 2, x), ("ctx_d", k))
        for rel in range(2):
            for d in (1, -1):
                recv(ctx_spot(k, (c + rel) % 2, (x + 2) % X, 0 if d == 1 else 1), ("ctx", k, rel, d, 2))

    for k in range(2):
        for rel in (1, 0):
            attend(k, rel)
    wo_event(2)
    y_event("B", 0, 1)
    for k in range(2, 4):
        for rel in (1, 0):
            attend(k, rel)
    wo_event(3)
    z_pass("B", 0, 1)
    z_event("A", 0, 1)
    z_start("A", 1)
    z_start("A", 2)
    ctx_pass(0)
    ctx_pass(1)
    z_event("A", -1, 1)
    wo_event(4)

    def stream_spot(k, cc, xx, half=None):
        row = (2 * k + cc) * 128
        rows = pl.ds(mult(row, 128), 128) if half is None else pl.ds(mult(row + half * 64, 64), 64)
        return stream.at[rows, pl.ds(mult(xx * 1024, 1024), 1024)]

    def project(k):
        rows = pl.ds(mult((2 * k + c) * 128, 128), 128)
        for block in range(4):
            part = jnp.dot(
                ctx_all[128 * k : 128 * k + 128, :], wo[:, 256 * block : 256 * block + 256], preferred_element_type=F32
            )
            part = part + res[k, :, 256 * block : 256 * block + 256].astype(F32)
            stream[rows, pl.ds(mult(x * 1024 + 256 * block, 256), 256)] = part.astype(BF16)
        ref = stream_spot(k, c, x)
        for d in (1, -1):
            send(ref, ref, dev(0, 0, d, 0), ("st", k, d, 1))
        send(ref, ref, dev(0, 0, 0, 1), ("st_d", k, 0, 0))

    def stream_pass(k, hop):
        for d in (1, -1):
            half = None if hop == 1 else (0 if d == 1 else 1)
            ref = stream_spot(k, c, (x - d * hop + X) % X, half)
            recv(ref, ("st", k, d, hop))
            if hop == 1:
                on = stream_spot(k, c, (x - d + X) % X, 0 if d == 1 else 1)
                send(on, on, dev(0, 0, d, 0), ("st", k, d, 2))
            send(ref, ref, dev(0, 0, 0, 1), ("st_d", k, d, hop))

    def stream_end(k):
        other = (c + 1) % 2
        recv(stream_spot(k, other, x), ("st_d", k, 0, 0))
        for hop in (1, 2):
            for d in (1, -1):
                half = None if hop == 1 else (0 if d == 1 else 1)
                recv(stream_spot(k, other, (x - d * hop + X) % X, half), ("st_d", k, d, hop))

    for dz, half in [(0, None), (-1, None), (1, None), (-2, None), (2, None), (-3, None), (3, None), (4, 0), (4, 1)]:
        recv(wo_block((z + dz + Z) % Z, (c + 1) % 2, half), ("wo_d", dz, half))
    for copy in res_loads:
        copy.wait()
    ctx_end(0)
    project(0)
    ctx_pass(2)
    ctx_end(1)
    project(1)
    ctx_pass(3)
    y_event("B", 0, 2)
    y_event("B", -1, 1)
    y_event("B", 1, 1)
    z_wait("B", 0, 2)
    z_pass("B", 0, 2)
    y_start("B", 2)
    y_start("B", -2)
    ctx_end(2)
    project(2)
    z_event("A", 0, 2)
    z_event("A", 1, 1)
    stream_pass(0, 1)
    ctx_end(3)
    project(3)
    z_event("A", 2, 1)
    z_event("A", -1, 2)
    y_event("B", -1, 2)
    y_event("B", 1, 2)
    stream_pass(1, 1)
    stream_pass(0, 2)
    z_event("B", 0, 3)
    y_start("B", 3)
    y_start("B", -3)
    z_event("A", 0, 3)
    z_event("A", 1, 2)
    z_event("A", 2, 2)
    y_event("B", 2, 1)
    y_event("B", -2, 1)
    stream_pass(2, 1)
    stream_pass(1, 2)
    z_event("A", -1, 3)
    z_event("B", 0, 4)
    y_start("B", 4)
    z_event("A", 1, 3)
    z_event("A", 2, 3)
    stream_pass(3, 1)
    stream_pass(2, 2)
    y_event("B", 2, 2)
    y_event("B", -2, 2)
    y_event("B", 3, 1)
    y_event("B", -3, 1)
    y_event("B", 4, 1)
    y_event("B", 3, 2)
    y_event("B", -3, 2)
    for dy in (0, -1, 1, 2):
        z_event("A", dy, 4)
    y_event("B", 4, 2)
    stream_pass(3, 2)

    outs = []

    def feed_forward(k):
        rows = pl.ds(256 * k, 256)

        def add_squares(i, total):
            piece = stream[rows, pl.ds(mult(i * 256, 256), 256)].astype(F32)
            piece = piece * piece
            return total + piece[:, :128] + piece[:, 128:]

        squares = lax.fori_loop(0, D // 256, add_squares, jnp.zeros((256, 128), F32))
        scale = lax.rsqrt(jnp.sum(squares, axis=1, keepdims=True) * (1.0 / D) + 1e-5)

        def one(block, _):
            both = jnp.dot(
                stream[rows, :], w[:, pl.ds(mult(block * 256, 256), 256)], preferred_element_type=F32
            )
            gate, up = both[:, :128] * scale, both[:, 128:] * scale
            hid[rows, pl.ds(mult(block * 128, 128), 128)] = (gate / (1.0 + jnp.exp(-gate)) * up).astype(BF16)
            return 0

        lax.fori_loop(0, N_BLOCKS, one, 0)
        both = jnp.dot(stream[rows, :], w[:, 256 * N_BLOCKS :], preferred_element_type=F32) * scale
        up = pltpu.roll(both, 128 - TAIL, 1)
        act = (both / (1.0 + jnp.exp(-both)) * up).astype(BF16)
        hid[rows, 128 * N_BLOCKS :] = act[:, :TAIL]
        outs.append(local(hid.at[rows], hidden.at[rows]))

    for k in range(4):
        stream_end(k)
        feed_forward(k)
    for yy in range(Y):
        for zz in range(Z):
            out_rows[:, zz * 512 + yy * 128 : zz * 512 + yy * 128 + 128] = stream[
                mine, yy * 1024 + zz * 128 : yy * 1024 + zz * 128 + 128
            ]
    outs.append(local(out_rows, resid_out))
    for copy in outs:
        copy.wait()
    for ahead in range(1, X):

        @pl.when((x + ahead) % X == y)
        def _(copy=gather[ahead]):
            copy.wait_send()

    @pl.when(collector)
    def _():
        for copy in spread:
            copy.wait_send()

    for copy in sent:
        copy.wait_send()
    assert state["send"] <= N_SEMS and len(recv_ids) <= N_SEMS


def body(queries, keys, values, spans, resid_in, out_weight, norm_gain, gate_weight, up_weight):
    anywhere = pl.BlockSpec(memory_space=pl.ANY)
    vmem = pl.BlockSpec(memory_space=pltpu.VMEM)
    smem = pl.BlockSpec(memory_space=pltpu.SMEM)
    return pl.pallas_call(
        kernel,
        out_shape=(jax.ShapeDtypeStruct((128, D), BF16), jax.ShapeDtypeStruct((SEQ, FF), BF16)),
        in_specs=[anywhere, anywhere, anywhere, smem, anywhere, vmem, vmem, vmem, vmem],
        out_specs=(anywhere, anywhere),
        scratch_shapes=[
            pltpu.VMEM((3, SEQ, 256), BF16),
            pltpu.VMEM((SEQ, 256), BF16),
            pltpu.VMEM((512, 2048), BF16),
            pltpu.VMEM((4, 128, 1024), BF16),
            pltpu.VMEM((SEQ, D), BF16),
            pltpu.VMEM((2048, 1024), BF16),
            pltpu.VMEM((D, WIDE), BF16),
            pltpu.VMEM((SEQ, FF), BF16),
            pltpu.VMEM((128, D), BF16),
            pltpu.SemaphoreType.DMA((N_SEMS,)),
            pltpu.SemaphoreType.DMA((N_SEMS,)),
            pltpu.SemaphoreType.DMA((32,)),
        ],
        compiler_params=pltpu.CompilerParams(
            collective_id=0, has_side_effects=True, vmem_limit_bytes=56 * 1024 * 1024
        ),
    )(
        queries, keys, values, spans, resid_in.reshape(4, 2, 128, D), out_weight,
        norm_gain.reshape(D // 128, 128), gate_weight, up_weight,
    )


def solution(mesh):
    return jax.shard_map(
        body,
        mesh=mesh,
        in_specs=(
            P(("dp", "ctx"), None),
            P(("dp", "ctx"), None),
            P(("dp", "ctx"), None),
            P("dp", None),
            P("dp", None),
            P("ctx", "dp"),
            P(),
            P("dp", "ctx"),
            P("dp", "ctx"),
        ),
        out_specs=(P(("dp", "ctx"), None), P("dp", "ctx")),
        check_vma=False,
    )
```

time: 408 us -> 165 us (0.40); the launches traced: 404 us -> 165 us
  waiting for transfers between devices: 304 us -> 0 us
  Pallas kernels: 0 us -> 157 us
  matrix products: 43.8 us -> 0 us
  other arithmetic: 18 us -> 0 us
  between operations: 15.1 us -> 0.65 us
  starting transfers between devices: 13.8 us -> 0 us
    all_gather x3 -> x0, waiting for transfers between devices: 172 us -> none  [the longest x1 79.4 us: body(): lax.all_gather(up_weight, 'dp', axis=0, tiled=True)]
    pallas_call x0 -> x1, Pallas kernels: none -> 157 us  [body(): pl.pallas_call(kernel, out_shape=(jax.ShapeDtypeStruct((128, D), BF16), j...]
    psum x1 -> x0, waiting for transfers between devices: 110 us -> none  [body(): lax.psum(partial_out.astype(jnp.bfloat16), 'ctx').astype(jnp.float32)]
    dot_general x5 -> x0, matrix products: 35.8 us -> none  [the longest x1 12.9 us: body(): jnp.dot(normed, lax.all_gather(up_weight, 'dp', axis=0, tiled=True), pref...]
    all_to_all x3 -> x0, waiting for transfers between devices: 20.3 us -> none  [the longest x1 7.61 us: body(): lax.all_to_all(keys, 'ctx', split_axis=1, concat_axis=0, tiled=True)]
    all_to_all x3 -> x0, starting transfers between devices: 13.5 us -> none  [the longest x1 4.97 us: body(): lax.all_to_all(keys, 'ctx', split_axis=1, concat_axis=0, tiled=True)]
    reduce_sum x1 -> x0, other arithmetic: 8.53 us -> none  [rms_normed(): scale = lax.rsqrt(jnp.mean(stream * stream, axis=-1, keepdims=True) + 1e-05)]
    sub x2 -> x0, matrix products: 8.04 us -> none  [block_softmax(): expo = jnp.where(allowed, jnp.exp(scores - peak), jnp.float32(0.0))]
  transfers between devices with their start and end apart: 7 -> 0, of which waited for: 7 -> 0; matrix products, arithmetic and copies ran while one was open for 13% -> 0% of each run, Pallas kernels for 0% -> 0%
where the time goes in v1:
time: 165 us
  Pallas kernels  157 us (95%)
  local copies, waits for them, and re-layouts  7.05 us (4%)
    pallas_call x1, Pallas kernels, body(): pl.pallas_call(kernel, out_shape=(jax.ShapeDtypeStruct((128, D), BF16), j...  157 us
    unnamed x5, local copies, waits for them, and re-layouts  4.44 us

profile of v1, /device:TPU:9, one launch (start us, length us, event | category | flops | bytes accessed | tf_op | source)
XLA Modules:
  0.0 165.2 jit_solution(2262303187045459894)
XLA Ops:
  0.6 1.7 %copy.11.gate_in = bf16[128,688]{1,0:T(8,128)(2,1)} copy(bf16[128,688]{0,1:T(8,128)(2,1)} %param.16) | data formatting | bytes 352256 | tf_op args[7]
  2.4 1.7 %copy.12.up_in = bf16[128,688]{1,0:T(8,128)(2,1)} copy(bf16[128,688]{0,1:T(8,128)(2,1)} %param.17) | data formatting | bytes 352256 | tf_op args[8]
  4.1 157.5 %shard_map.104 = (bf16[128,4096]{1,0:T(8,128)(2,1)}, bf16[1024,688]{1,0:T(8,128)(2,1)}) custom-call(bf16[128,2048]{1,0:T(8,128)(2,1)} %q_in.1, bf16[128,2048]{1,0:T(8,128)(2,1)} %k_in.1, bf16[128,2048]{1,0:T(8,128)(2,1)} %v_in.1, s32[1,2]{1,0:T(1,128)} %spans.1, bf16[4,2,128,4096]{3,2,1,0:T(8,128)(2,1)} %bitcast.2, bf16[256,128]{1,0:T(8,128)(2,1)} %wo_in.1, ...), custom_call_target="tpu_custom_call" | custom-call | tf_op jit(solution)/shard_map/pallas_call | solution.py:462
  161.6 0.0 copy-start
  161.6 2.6 %copy.13 = bf16[1024,688]{0,1:T(8,128)(2,1)} copy(bf16[1024,688]{1,0:T(8,128)(2,1)} %get-tuple-element.3) | data formatting | bytes 2818048 | tf_op jit(solution)/shard_map/pallas_call | solution.py:462
  164.2 0.0 copy-done
  164.2 1.0 copy.15
Async XLA Ops:
  161.6 2.6 %copy-start = (bf16[128,4096]{1,0:T(8,128)(2,1)S(1)}, bf16[128,4096]{1,0:T(8,128)(2,1)}, u32[]{:S(2)}) copy-start(bf16[128,4096]{1,0:T(8,128)(2,1)} %get-tuple-element.6) | copy-start | bytes 3145732

commit v2 on v1

v2 whole, which is shorter than its diff:
```python
import functools
import math

import jax
import jax.numpy as jnp
from jax import lax
from jax.experimental import pallas as pl
from jax.experimental.pallas import tpu as pltpu
from jax.sharding import PartitionSpec as P

MESH = pl.DeviceIdType.MESH
Z, Y, X = 8, 4, 4
HD = 128
SEQ, D, FF = 1024, 4096, 688
PART_ROWS = {"A": (0, 512), "B": (512, 2 * FF - 512)}
EXP2_SCALE = math.log2(math.e) / math.sqrt(HD)
F32, BF16 = jnp.float32, jnp.bfloat16
N_SEMS = 256


def mult(value, of):
    return pl.multiple_of(value, of)


def kernel(
    q_in, k_in, v_in, spans, resid, wo_in, gain, gate_in, up_in,
    resid_out, hidden,
    qkv, ctx_own, ctx_all, res, stream, wo, w, acc, scales, hid,
    send_sem, recv_sem, local_sem,
):
    cx, dp = lax.axis_index("ctx"), lax.axis_index("dp")
    x, c = cx // 2, cx % 2
    z, y = dp // Y, dp % Y

    def dev(dz=0, dy=0, dx=0, dc=0):
        zz, yy = (z + dz + Z) % Z, (y + dy + Y) % Y
        xx, cc = (x + dx + X) % X, (c + dc) % 2
        return (zz * Y + yy, xx * 2 + cc)

    recv_ids, sent, state = {}, [], {"send": 0, "local": 0, "drained": 0}

    def recv_id(key):
        return recv_ids.setdefault(key, len(recv_ids))

    def send(src, dst, target, key, when=None):
        index = state["send"]
        state["send"] += 1
        copy = pltpu.make_async_remote_copy(
            src_ref=src, dst_ref=dst, send_sem=send_sem.at[index], recv_sem=recv_sem.at[recv_id(key)],
            device_id=target, device_id_type=MESH,
        )
        copy.start()
        if when is None:
            sent.append(copy)
        return copy

    def recv(dst, key):
        pltpu.make_async_remote_copy(
            src_ref=dst, dst_ref=dst, send_sem=send_sem.at[0], recv_sem=recv_sem.at[recv_id(key)],
            device_id=dev(0, 0, 0, 1), device_id_type=MESH,
        ).wait_recv()

    def drain(count):
        for copy in sent[state["drained"] : count]:
            copy.wait_send()
        state["drained"] = max(count, state["drained"])

    def local(src, dst):
        copy = pltpu.make_async_copy(src, dst, local_sem.at[state["local"]])
        state["local"] += 1
        copy.start()
        return copy

    barrier = pltpu.get_barrier_semaphore()
    peers = [(0, 0, dx, dc) for dx in range(X) for dc in range(2) if (dx, dc) != (0, 0)]
    peers += [(0, 1, 0, 0), (0, 2, 0, 0), (0, 3, 0, 0), (1, 0, 0, 0), (-1, 0, 0, 0)]
    for peer in peers:
        pl.semaphore_signal(barrier, inc=1, device_id=dev(*peer), device_id_type=MESH)
    pl.semaphore_wait(barrier, len(peers))

    def wo_block(zz, cc, unit=None):
        rows = pl.ds(mult(cc * 1024, 1024), 1024) if unit is None else pl.ds(mult(cc * 1024 + unit * 512, 512), 512)
        return wo.at[rows, pl.ds(mult((zz + Z) % Z * 128, 128), 128)]

    def wo_rows(xx):
        return wo.at[pl.ds(mult(c * 1024 + xx * 256, 256), 256), pl.ds(mult(z * 128, 128), 128)]

    collector = x == y
    gather = {}
    wo_first = state["send"]
    state["send"] += 7
    for ahead in range(1, X):
        gather[ahead] = pltpu.make_async_remote_copy(
            src_ref=wo_in, dst_ref=wo_rows(x), send_sem=send_sem.at[wo_first],
            recv_sem=recv_sem.at[recv_id(("wo_x", ahead))], device_id=dev(0, 0, ahead, 0), device_id_type=MESH,
        )

        @pl.when((x + ahead) % X == y)
        def _(copy=gather[ahead]):
            copy.start()

    mine = pl.ds(mult(cx * 128, 128), 128)
    shares = [(1, k_in), (2, v_in), (0, q_in)]
    order = [(dx, dc) for dx in (2, 1, 3, 0) for dc in range(2) if (dx, dc) != (0, 0)]
    for which, source in shares:
        for dx, dc in order:
            target = dev(0, 0, dx, dc)
            columns = pl.ds(mult(target[1] * 256, 256), 256)
            send(source.at[:, columns], qkv.at[which, mine], target, ("qkv", which, dx, dc))
    own_columns = pl.ds(mult(cx * 256, 256), 256)
    loads = [local(source.at[:, own_columns], qkv.at[which, mine]) for which, source in shares]

    def pack_own():
        gain_row = gain[pl.ds(dp, 1), :]
        columns = pl.ds(mult(y * 128, 128), 128)
        w[z, :FF, columns] = (gate_in[...].astype(F32) * gain_row).astype(BF16)
        w[z, FF:, columns] = (up_in[...].astype(F32) * gain_row).astype(BF16)

    pack_own()

    def w_block(part, dz, dy, half=None):
        first, count = PART_ROWS[part]
        if half is not None:
            first, count = first + half * count // 2, count // 2
        return w.at[(z + dz + Z) % Z, first : first + count, pl.ds(mult((y + dy + Y) % Y * 128, 128), 128)]

    def z_send(part, dz, dy, d, key, half=None):
        ref = w_block(part, dz, dy, half)
        send(ref, ref, dev(d, 0, 0, 0), key)

    def y_send(part, dz, dy, d, key, half=None):
        ref = w_block(part, dz, dy, half)
        send(ref, ref, dev(0, d, 0, 0), key)

    def z_start(part, dy):
        for d in (1, -1):
            z_send(part, 0, dy, d, (part, "z", dy, d, 1))

    def z_wait(part, dy, hop):
        for d in (1, -1):
            half = None if hop < 4 else (0 if d == 1 else 1)
            recv(w_block(part, -d * hop, dy, half), (part, "z", dy, d, hop))

    def z_pass(part, dy, hop):
        for d in (1, -1):
            half = None if hop < 3 else (0 if d == 1 else 1)
            z_send(part, -d * hop, dy, d, (part, "z", dy, d, hop + 1), half)

    def z_event(part, dy, hop):
        z_wait(part, dy, hop)
        if hop < 4:
            z_pass(part, dy, hop)

    def y_start(part, dz):
        for d in (1, -1):
            y_send(part, dz, 0, d, (part, "y", dz, d, 1))

    def y_event(part, dz, hop):
        for d in (1, -1):
            half = None if hop < 2 else (0 if d == 1 else 1)
            recv(w_block(part, dz, -d * hop, half), (part, "y", dz, d, hop))
            if hop == 1:
                half = 0 if d == 1 else 1
                y_send(part, dz, -d, d, (part, "y", dz, d, 2), half)

    z_start("B", 0)
    z_start("A", 0)

    @pl.when(collector)
    def _():
        for ahead in range(1, X):
            recv(wo_rows((x - ahead + X) % X), ("wo_x", ahead))
        wo[pl.ds(mult(c * 1024 + x * 256, 256), 256), pl.ds(mult(z * 128, 128), 128)] = wo_in[...]

    spread = []
    for unit in range(2):
        for ahead in range(1, Y):
            spread.append(
                pltpu.make_async_remote_copy(
                    src_ref=wo_block(z, c, unit), dst_ref=wo_block(z, c, unit),
                    send_sem=send_sem.at[wo_first + 1 + len(spread)], recv_sem=recv_sem.at[recv_id(("wo_y", unit))],
                    device_id=dev(0, ahead, 0, 0), device_id_type=MESH,
                )
            )

            @pl.when(collector)
            def _(copy=spread[-1]):
                copy.start()

    def wo_y_wait(unit):
        @pl.when(jnp.logical_not(collector))
        def _():
            recv(wo_block(z, c, unit), ("wo_y", unit))

    def wo_across(dz, unit):
        ref = wo_block(z + dz, c, unit)
        send(ref, ref, dev(0, 0, 0, 1), ("wo_d", dz, unit))

    def wo_start(unit):
        ref = wo_block(z, c, unit)
        for d in (1, -1):
            send(ref, ref, dev(d, 0, 0, 0), ("wo_z", unit, d, 1))
        wo_across(0, unit)

    def wo_event(unit, hop):
        for d in (1, -1):
            if hop == 4 and unit != (0 if d == 1 else 1):
                continue
            ref = wo_block(z - d * hop, c, unit)
            recv(ref, ("wo_z", unit, d, hop))
            if hop < 3 or (hop == 3 and unit == (0 if d == 1 else 1)):
                send(ref, ref, dev(d, 0, 0, 0), ("wo_z", unit, d, hop + 1))
            wo_across(4 if hop == 4 else -d * hop, unit)

    def wo_d_wait():
        for dz in (0, -1, 1, -2, 2, -3, 3, 4):
            for unit in range(2):
                recv(wo_block(z + dz, (c + 1) % 2, unit), ("wo_d", dz, unit))

    def qkv_wait():
        for copy in loads:
            copy.wait()
        for which, _ in shares:
            for dx, dc in order:
                rows = pl.ds(mult(dev(0, 0, -dx, dc)[1] * 128, 128), 128)
                recv(qkv.at[which, rows], ("qkv", which, dx, dc))

    prefix_end, middle_end = spans[0, 0], spans[0, 1]

    def ranks(pos):
        late = prefix_end + (SEQ - middle_end) + (pos - prefix_end)
        return jnp.where(pos < prefix_end, pos, jnp.where(pos >= middle_end, prefix_end + pos - middle_end, late))

    key_rank = ranks(lax.broadcasted_iota(jnp.int32, (1, SEQ), 1))

    def ctx_spot(k, cc, xx, half=None):
        rows = pl.ds(128 * k, 128) if half is None else pl.ds(128 * k + 64 * half, 64)
        return ctx_all.at[rows, pl.ds(mult(cc * 1024 + xx * 256, 256), 256)]

    def attend(k, rel):
        row = mult((2 * k + (c + rel) % 2) * 128, 128)
        rows = pl.ds(row, 128)
        query_rank = ranks(row + lax.broadcasted_iota(jnp.int32, (128, 1), 0))
        allowed = query_rank >= key_rank
        for head in range(2):
            cols = slice(head * HD, head * HD + HD)
            scores = lax.dot_general(
                qkv[0, rows, cols], qkv[1, :, cols], (((1,), (1,)), ((), ())), preferred_element_type=F32
            )
            scores = jnp.where(allowed, scores, -jnp.inf)
            peak = jnp.max(scores, axis=1, keepdims=True)
            expo = jnp.exp2((scores - peak) * EXP2_SCALE)
            total = jnp.sum(expo, axis=1, keepdims=True)
            mixed = jnp.dot(expo.astype(BF16), qkv[2, :, cols], preferred_element_type=F32)
            mixed = (mixed / total).astype(BF16)
            ctx_own[rows, cols] = mixed
            if rel == 0:
                ctx_all[128 * k : 128 * k + 128, pl.ds(mult(c * 1024 + x * 256 + head * HD, 128), HD)] = mixed
        for d in (1, -1):
            send(ctx_own.at[rows], ctx_spot(k, c, x), dev(0, 0, d, rel), ("ctx", k, rel, d, 1))
        if rel == 1:
            send(ctx_own.at[rows], ctx_spot(k, c, x), dev(0, 0, 0, 1), ("ctx_d", k))

    def ctx_pass(k):
        for rel in range(2):
            cc = (c + rel) % 2
            for d in (1, -1):
                recv(ctx_spot(k, cc, (x - d + X) % X), ("ctx", k, rel, d, 1))
                ref = ctx_spot(k, cc, (x - d + X) % X, 0 if d == 1 else 1)
                send(ref, ref, dev(0, 0, d, 0), ("ctx", k, rel, d, 2))

    def ctx_end(k):
        recv(ctx_spot(k, (c + 1) % 2, x), ("ctx_d", k))
        for rel in range(2):
            for d in (1, -1):
                recv(ctx_spot(k, (c + rel) % 2, (x + 2) % X, 0 if d == 1 else 1), ("ctx", k, rel, d, 2))

    res_loads = []
    for zz in range(Z):
        columns = pl.ds(mult(zz * 512 + x * 128, 128), 128)
        res_loads.append(local(resid.at[:, c, :, columns], res.at[:, :, pl.ds(zz * 128, 128)]))

    def stream_spot(k, cc, xx, half=None):
        row = (2 * k + cc) * 128
        rows = pl.ds(mult(row, 128), 128) if half is None else pl.ds(mult(row + half * 64, 64), 64)
        return stream.at[:, rows, pl.ds(mult(xx * 128, 128), 128)]

    def project(k):
        rows = pl.ds(mult((2 * k + c) * 128, 128), 128)
        columns = pl.ds(mult(x * 128, 128), 128)
        for block in range(4):
            part = jnp.dot(
                ctx_all[128 * k : 128 * k + 128, :], wo[:, 256 * block : 256 * block + 256], preferred_element_type=F32
            )
            part = part + res[k, :, 256 * block : 256 * block + 256].astype(F32)
            stream[2 * block, rows, columns] = part[:, :128].astype(BF16)
            stream[2 * block + 1, rows, columns] = part[:, 128:].astype(BF16)
        ref = stream_spot(k, c, x)
        for d in (1, -1):
            send(ref, ref, dev(0, 0, d, 0), ("st", k, d, 1))
        send(ref, ref, dev(0, 0, 0, 1), ("st_d", k, 0, 0))

    def stream_pass(k, hop):
        for d in (1, -1):
            half = None if hop == 1 else (0 if d == 1 else 1)
            ref = stream_spot(k, c, (x - d * hop + X) % X, half)
            recv(ref, ("st", k, d, hop))
            if hop == 1:
                on = stream_spot(k, c, (x - d + X) % X, 0 if d == 1 else 1)
                send(on, on, dev(0, 0, d, 0), ("st", k, d, 2))
            send(ref, ref, dev(0, 0, 0, 1), ("st_d", k, d, hop))

    def stream_end(k):
        other = (c + 1) % 2
        recv(stream_spot(k, other, x), ("st_d", k, 0, 0))
        for hop in (1, 2):
            for d in (1, -1):
                half = None if hop == 1 else (0 if d == 1 else 1)
                recv(stream_spot(k, other, (x - d * hop + X) % X, half), ("st_d", k, d, hop))

    outs = []

    def norm_scale(k):
        rows = pl.ds(256 * k, 256)

        def add_squares(i, total):
            piece = stream[i, rows, :].astype(F32)
            piece = piece * piece
            return total + (piece[:, :128] + piece[:, 128:256]) + (piece[:, 256:384] + piece[:, 384:])

        squares = lax.fori_loop(0, Z, add_squares, jnp.zeros((256, 128), F32))
        total = jnp.sum(squares.T, axis=0, keepdims=True)
        scales[k] = lax.rsqrt(total * (1.0 / D) + 1e-5)

    def ff_part(k, *dzs):
        rows = slice(256 * k, 256 * k + 256)

        def one(half, _):
            at = pl.ds(mult(half * FF, 16), FF)
            total = None
            for dz in dzs:
                zz = (z + dz + Z) % Z
                part = lax.dot_general(
                    w[zz, at, :], stream[zz, rows, :], (((1,), (1,)), ((), ())), preferred_element_type=F32
                )
                total = part if total is None else total + part
            acc[at, rows] = total if 0 in dzs else acc[at, rows] + total
            return 0

        lax.fori_loop(0, 2, one, 0)

    def activate(k):
        rows = slice(256 * k, 256 * k + 256)
        scale = scales[k]
        for first in range(0, FF, 128):
            count = min(128, FF - first)
            gate = acc[first : first + count, rows] * scale
            up = acc[FF + first : FF + first + count, rows] * scale
            hid[first : first + count, rows] = (gate / (1.0 + jnp.exp(-gate)) * up).astype(BF16)
        outs.append(local(hid.at[:, rows], hidden.at[:, rows]))

    y_start("A", 0)
    y_event("A", 0, 1)
    z_start("A", -1)
    for unit in range(2):
        wo_y_wait(unit)
        wo_start(unit)
    y_start("B", 0)
    y_event("A", 0, 2)
    z_wait("B", 0, 1)
    y_start("B", 1)
    y_start("B", -1)
    wo_event(0, 1)
    wo_event(1, 1)
    qkv_wait()
    attend(0, 1)
    attend(0, 0)
    wo_event(0, 2)
    attend(1, 1)
    attend(1, 0)
    wo_event(1, 2)
    attend(2, 1)
    attend(2, 0)
    attend(3, 1)
    attend(3, 0)
    wo_event(0, 3)
    ctx_pass(0)
    wo_event(1, 3)
    z_pass("B", 0, 1)
    z_event("A", 0, 1)
    z_start("A", 1)
    z_start("A", 2)
    ctx_pass(1)
    y_event("B", 0, 1)
    ctx_pass(2)
    wo_event(0, 4)
    wo_event(1, 4)
    ctx_pass(3)
    for copy in res_loads:
        copy.wait()
    wo_d_wait()
    for k in range(4):
        ctx_end(k)
        project(k)
        if k == 0:
            z_event("A", -1, 1)
        if k == 1:
            y_event("B", 0, 2)
            y_event("B", -1, 1)
            y_event("B", 1, 1)
    z_event("B", 0, 2)
    y_start("B", 2)
    y_start("B", -2)
    z_event("A", 0, 2)
    z_event("A", 1, 1)
    z_event("A", 2, 1)
    stream_pass(0, 1)
    z_event("A", -1, 2)
    y_event("B", -1, 2)
    y_event("B", 1, 2)
    stream_pass(1, 1)
    stream_pass(0, 2)
    z_event("B", 0, 3)
    y_start("B", 3)
    y_start("B", -3)
    z_event("A", 0, 3)
    z_event("A", 1, 2)
    z_event("A", 2, 2)
    y_event("B", 2, 1)
    y_event("B", -2, 1)
    stream_pass(2, 1)
    stream_pass(1, 2)
    stream_end(0)
    norm_scale(0)
    ff_part(0, 0, 1, -1)
    z_event("A", -1, 3)
    z_event("B", 0, 4)
    y_start("B", 4)
    z_event("A", 1, 3)
    z_event("A", 2, 3)
    stream_pass(3, 1)
    stream_pass(2, 2)
    stream_end(1)
    norm_scale(1)
    ff_part(1, 0, 1, -1)
    y_event("B", 2, 2)
    y_event("B", -2, 2)
    ff_part(0, 2, -2)
    ff_part(1, 2, -2)
    y_event("B", 3, 1)
    y_event("B", -3, 1)
    y_event("B", 4, 1)
    stream_pass(3, 2)
    stream_end(2)
    norm_scale(2)
    ff_part(2, 0, 1, -1)
    ff_part(2, 2, -2)
    stream_end(3)
    norm_scale(3)
    for zz in range(Z):
        outs.append(local(stream.at[zz, mine, :], resid_out.at[:, 512 * zz : 512 * zz + 512]))
    ff_part(3, 0, 1, -1)
    ff_part(3, 2, -2)
    y_event("B", 3, 2)
    y_event("B", -3, 2)
    for k in range(4):
        ff_part(k, 3, -3)
    drain(len(sent))
    for dy in (0, -1, 1, 2):
        z_event("A", dy, 4)
    y_event("B", 4, 2)
    for k in range(4):
        ff_part(k, 4)
        activate(k)

    def final_wait():
        for copy in outs:
            copy.wait()
        for ahead in range(1, X):

            @pl.when((x + ahead) % X == y)
            def _(copy=gather[ahead]):
                copy.wait_send()

        @pl.when(collector)
        def _():
            for copy in spread:
                copy.wait_send()

        drain(len(sent))

    final_wait()
    assert state["send"] <= N_SEMS and len(recv_ids) <= N_SEMS


def body(queries, keys, values, spans, resid_in, out_weight, norm_gain, gate_weight, up_weight):
    anywhere = pl.BlockSpec(memory_space=pl.ANY)
    vmem = pl.BlockSpec(memory_space=pltpu.VMEM)
    smem = pl.BlockSpec(memory_space=pltpu.SMEM)
    resid_out, hidden = pl.pallas_call(
        kernel,
        out_shape=(jax.ShapeDtypeStruct((128, D), BF16), jax.ShapeDtypeStruct((FF, SEQ), BF16)),
        in_specs=[anywhere, anywhere, anywhere, smem, anywhere, vmem, vmem, vmem, vmem],
        out_specs=(anywhere, anywhere),
        scratch_shapes=[
            pltpu.VMEM((3, SEQ, 256), BF16),
            pltpu.VMEM((SEQ, 256), BF16),
            pltpu.VMEM((512, 2048), BF16),
            pltpu.VMEM((4, 128, 1024), BF16),
            pltpu.VMEM((Z, SEQ, 512), BF16),
            pltpu.VMEM((2048, 1024), BF16),
            pltpu.VMEM((Z, 2 * FF, 512), BF16),
            pltpu.VMEM((2 * FF, SEQ), F32),
            pltpu.VMEM((4, 1, 256), F32),
            pltpu.VMEM((FF, SEQ), BF16),
            pltpu.SemaphoreType.DMA((N_SEMS,)),
            pltpu.SemaphoreType.DMA((N_SEMS,)),
            pltpu.SemaphoreType.DMA((32,)),
        ],
        compiler_params=pltpu.CompilerParams(
            collective_id=0, has_side_effects=True, vmem_limit_bytes=56 * 1024 * 1024
        ),
    )(
        queries, keys, values, spans, resid_in.reshape(4, 2, 128, D), out_weight,
        norm_gain.reshape(D // 128, 128), gate_weight.T, up_weight.T,
    )
    return resid_out, hidden.T


def solution(mesh):
    return jax.shard_map(
        body,
        mesh=mesh,
        in_specs=(
            P(("dp", "ctx"), None),
            P(("dp", "ctx"), None),
            P(("dp", "ctx"), None),
            P("dp", None),
            P("dp", None),
            P("ctx", "dp"),
            P(),
            P("dp", "ctx"),
            P("dp", "ctx"),
        ),
        out_specs=(P(("dp", "ctx"), None), P("dp", "ctx")),
        check_vma=False,
    )
```

time: 165 us -> 138 us (0.84)
  Pallas kernels: 157 us -> 134 us
  local copies, waits for them, and re-layouts: 7.05 us -> 3.49 us
    pallas_call x1, Pallas kernels: 157 us -> 134 us  [body(): pl.pallas_call(kernel, out_shape=(jax.ShapeDtypeStruct((128, D), BF16), j...]
    pallas_call x1 -> x0, local copies, waits for them, and re-layouts: 2.61 us -> none  [body(): pl.pallas_call(kernel, out_shape=(jax.ShapeDtypeStruct((128, D), BF16), j...]
    unnamed x5 -> x4, local copies, waits for them, and re-layouts: 4.44 us -> 3.49 us
where the time goes in v2:
time: 138 us
  Pallas kernels  134 us (97%)
  local copies, waits for them, and re-layouts  3.49 us (3%)
    pallas_call x1, Pallas kernels, body(): pl.pallas_call(kernel, out_shape=(jax.ShapeDtypeStruct((128, D), BF16), j...  134 us
    unnamed x4, local copies, waits for them, and re-layouts  3.49 us

profile of v2, /device:TPU:9, one launch (start us, length us, event | category | flops | bytes accessed | tf_op | source)
XLA Modules:
  0.0 138.0 jit_solution(1198443085071534054)
XLA Ops:
  0.6 133.9 %shard_map.104 = (bf16[128,4096]{1,0:T(8,128)(2,1)}, bf16[688,1024]{1,0:T(8,128)(2,1)}) custom-call(bf16[128,2048]{1,0:T(8,128)(2,1)} %q_in.1, bf16[128,2048]{1,0:T(8,128)(2,1)} %k_in.1, bf16[128,2048]{1,0:T(8,128)(2,1)} %v_in.1, s32[1,2]{1,0:T(1,128)} %spans.1, bf16[4,2,128,4096]{3,2,1,0:T(8,128)(2,1)} %bitcast.5, bf16[256,128]{1,0:T(8,128)(2,1)} %wo_in.1, ...), custom_call_target="tpu_custom_call" | custom-call | tf_op jit(solution)/shard_map/pallas_call | solution.py:500
  134.5 0.0 copy-start
  134.5 2.4 %copy.13 = bf16[128,4096]{1,0:T(8,128)(2,1)} copy(bf16[128,4096]{1,0:T(8,128)(2,1)} %get-tuple-element.8) | data formatting | bytes 2097152
  136.9 0.0 copy-done
  136.9 1.1 copy.14
Async XLA Ops:
  134.5 2.4 %copy-start = (bf16[688,1024]{1,0:T(8,128)(2,1)S(1)}, bf16[688,1024]{1,0:T(8,128)(2,1)}, u32[]{:S(2)}) copy-start(bf16[688,1024]{1,0:T(8,128)(2,1)} %get-tuple-element.5) | copy-start | bytes 4227076

commit v3 on v2

v3 whole, which is shorter than its diff:
```python
import functools
import math

import jax
import jax.numpy as jnp
from jax import lax
from jax.experimental import pallas as pl
from jax.experimental.pallas import tpu as pltpu
from jax.sharding import PartitionSpec as P

MESH = pl.DeviceIdType.MESH
Z, Y, X = 8, 4, 4
HD = 128
SEQ, D, FF = 1024, 4096, 688
PART_ROWS = {"A": (0, 512), "B": (512, 2 * FF - 512)}
EXP2_SCALE = math.log2(math.e) / math.sqrt(HD)
F32, BF16 = jnp.float32, jnp.bfloat16
VMEM_BYTES = 56 * 1024 * 1024
N_SEND, N_RECV, N_LOCAL = 11, 73, 9


def mult(value, of):
    return pl.multiple_of(value, of)


def kernel(
    q_in, k_in, v_in, spans_in, resid, wo_in, gain_in, gate_hbm, up_hbm,
    resid_out, hidden,
    qkv, ctx_own, ctx_all, res, stream, wo, w, acc, scales, hid, gain, gate_in, up_in, spans,
    send_sem, recv_sem, local_sem,
):
    cx, dp = lax.axis_index("ctx"), lax.axis_index("dp")
    x, c = cx // 2, cx % 2
    z, y = dp // Y, dp % Y

    def dev(dz=0, dy=0, dx=0, dc=0):
        zz, yy = (z + dz + Z) % Z, (y + dy + Y) % Y
        xx, cc = (x + dx + X) % X, (c + dc) % 2
        return (zz * Y + yy, xx * 2 + cc)

    send_ids, recv_ids, local_ids = {}, {}, {}

    def remote(src, dst, target, kind, event):
        return pltpu.make_async_remote_copy(
            src_ref=src, dst_ref=dst, send_sem=send_sem.at[send_ids.setdefault(kind, len(send_ids))],
            recv_sem=recv_sem.at[recv_ids.setdefault(event, len(recv_ids))], device_id=target, device_id_type=MESH,
        )

    def send(src, dst, target, kind, event):
        remote(src, dst, target, kind, event).start()

    def recv(as_large, event):
        remote(as_large, as_large, dev(0, 0, 0, 1), "qkv", event).wait_recv()

    def sent(as_large, kind):
        remote(as_large, as_large, dev(0, 0, 0, 1), kind, "q").wait_send()

    def local(src, dst, kind):
        index = local_ids.setdefault(kind, len(local_ids))
        pltpu.make_async_copy(src, dst, local_sem.at[index]).start()

    def local_wait(as_large, kind):
        pltpu.make_async_copy(as_large, as_large, local_sem.at[local_ids[kind]]).wait()

    local(gate_hbm, gate_in, "gate")
    local(up_hbm, up_in, "up")
    local(gain_in.at[pl.ds(dp, 1), :], gain, "gain")
    local(spans_in, spans, "spans")

    barrier = pltpu.get_barrier_semaphore()
    peers = [(0, 0, dx, dc) for dx in range(X) for dc in range(2) if (dx, dc) != (0, 0)]
    peers += [(0, 1, 0, 0), (0, 2, 0, 0), (0, 3, 0, 0), (1, 0, 0, 0), (-1, 0, 0, 0)]
    for peer in peers:
        pl.semaphore_signal(barrier, inc=1, device_id=dev(*peer), device_id_type=MESH)
    pl.semaphore_wait(barrier, len(peers))

    def wo_block(zz, cc, unit=None):
        rows = pl.ds(mult(cc * 1024, 1024), 1024) if unit is None else pl.ds(mult(cc * 1024 + unit * 512, 512), 512)
        return wo.at[rows, pl.ds(mult((zz + Z) % Z * 128, 128), 128)]

    def wo_rows(xx):
        return wo.at[pl.ds(mult(c * 1024 + xx * 256, 256), 256), pl.ds(mult(z * 128, 128), 128)]

    ahead = (y - x + X) % X
    collector = ahead == 0

    @pl.when(jnp.logical_not(collector))
    def _():
        send(wo_in, wo_rows(x), dev(0, 0, ahead, 0), "wo_x", "wo_x")

    def pack_own():
        local_wait(gate_in, "gate")
        local_wait(up_in, "up")
        local_wait(gain, "gain")
        gain_row = gain[...]
        columns = pl.ds(mult(y * 128, 128), 128)
        w[z, :FF, columns] = (gate_in[...].astype(F32) * gain_row).astype(BF16)
        w[z, FF:, columns] = (up_in[...].astype(F32) * gain_row).astype(BF16)

    pack_own()

    def w_block(part, dz, dy, half=None):
        first, count = PART_ROWS[part]
        if half is not None:
            first, count = first + half * count // 2, count // 2
        return w.at[(z + dz + Z) % Z, first : first + count, pl.ds(mult((y + dy + Y) % Y * 128, 128), 128)]

    def w_like(part, z_blocks, y_blocks):
        first, count = PART_ROWS[part]
        return w.at[:z_blocks, first : first + count, : 128 * y_blocks]

    def z_send(part, dz, dy, d, hop, half=None):
        ref = w_block(part, dz, dy, half)
        send(ref, ref, dev(d, 0, 0, 0), (part, "z"), (part, "z", dy, hop))

    def y_send(part, dz, dy, d, hop, half=None):
        ref = w_block(part, dz, dy, half)
        send(ref, ref, dev(0, d, 0, 0), (part, "y"), (part, "y", dz, hop))

    def z_start(part, dy):
        for d in (1, -1):
            z_send(part, 0, dy, d, 1)

    def z_wait(part, dy, hop):
        recv(w_like(part, 2 if hop < 4 else 1, 1), (part, "z", dy, hop))

    def z_pass(part, dy, hop):
        for d in (1, -1):
            half = None if hop < 3 else (0 if d == 1 else 1)
            z_send(part, -d * hop, dy, d, hop + 1, half)

    def z_event(part, dy, hop):
        z_wait(part, dy, hop)
        if hop < 4:
            z_pass(part, dy, hop)

    def y_start(part, dz):
        for d in (1, -1):
            y_send(part, dz, 0, d, 1)

    def y_event(part, dz, hop):
        recv(w_like(part, 2 if hop < 2 else 1, 1), (part, "y", dz, hop))
        if hop == 1:
            for d in (1, -1):
                y_send(part, dz, -d, d, 2, 0 if d == 1 else 1)

    y_start("A", 0)
    z_start("B", 0)
    z_start("A", 0)

    mine = pl.ds(mult(cx * 128, 128), 128)
    shares = {"k": (1, k_in), "v": (2, v_in), "q": (0, q_in)}

    def share(name):
        which, source = shares[name]
        for dx, dc in [(2, 0), (2, 1), (1, 0), (1, 1), (3, 0), (3, 1), (0, 1)]:
            target = dev(0, 0, dx, dc)
            columns = pl.ds(mult(target[1] * 256, 256), 256)
            send(source.at[:, columns], qkv.at[which, mine], target, "qkv", name)
        local(source.at[:, pl.ds(mult(cx * 256, 256), 256)], qkv.at[which, mine], "qkv")

    share("k")

    @pl.when(collector)
    def _():
        recv(wo.at[:256, :384], "wo_x")
        own_part = pltpu.make_async_copy(wo_in, wo_rows(x), local_sem.at[local_ids.setdefault("wo", len(local_ids))])
        own_part.start()
        own_part.wait()
        for unit in range(2):
            for d in (1, -1):
                ref = wo_block(z, c, unit)
                send(ref, ref, dev(0, d, 0, 0), "wo_y", ("wo_y", unit))

    def wo_y_wait(unit):
        @pl.when(jnp.logical_not(collector))
        def _():
            recv(wo_block(z, c, unit), ("wo_y", unit))

        d = 1 if unit == 0 else -1

        @pl.when(ahead == d % Y)
        def _():
            ref = wo_block(z, c, unit)
            send(ref, ref, dev(0, d, 0, 0), "wo_y", ("wo_y", unit))

    def wo_across(dz, unit):
        ref = wo_block(z + dz, c, unit)
        send(ref, ref, dev(0, 0, 0, 1), "wo_d", "wo_d")

    def wo_start(unit):
        ref = wo_block(z, c, unit)
        for d in (1, -1):
            send(ref, ref, dev(d, 0, 0, 0), "wo_z", ("wo_z", unit, 1))
        wo_across(0, unit)

    def wo_event(unit, hop):
        recv(wo_block(0, 0, 0) if hop == 4 else wo.at[:512, :256], ("wo_z", unit, hop))
        for d in (1, -1):
            if hop == 4 and unit != (0 if d == 1 else 1):
                continue
            ref = wo_block(z - d * hop, c, unit)
            if hop < 3 or (hop == 3 and unit == (0 if d == 1 else 1)):
                send(ref, ref, dev(d, 0, 0, 0), "wo_z", ("wo_z", unit, hop + 1))
            wo_across(4 if hop == 4 else -d * hop, unit)

    def wo_d_wait():
        recv(wo.at[:1024, :], "wo_d")

    def qkv_wait():
        local_wait(qkv.at[:, :128, :], "qkv")
        for name in shares:
            recv(qkv.at[0, :896], name)

    local_wait(spans, "spans")
    prefix_end, middle_end = spans[0, 0], spans[0, 1]

    def ranks(pos):
        late = prefix_end + (SEQ - middle_end) + (pos - prefix_end)
        return jnp.where(pos < prefix_end, pos, jnp.where(pos >= middle_end, prefix_end + pos - middle_end, late))

    key_rank = ranks(lax.broadcasted_iota(jnp.int32, (1, SEQ), 1))

    def ctx_spot(k, cc, xx, half=None):
        rows = pl.ds(128 * k, 128) if half is None else pl.ds(128 * k + 64 * half, 64)
        return ctx_all.at[rows, pl.ds(mult(cc * 1024 + xx * 256, 256), 256)]

    def attend(k, rel):
        row = mult((2 * k + (c + rel) % 2) * 128, 128)
        rows = pl.ds(row, 128)
        query_rank = ranks(row + lax.broadcasted_iota(jnp.int32, (128, 1), 0))
        allowed = query_rank >= key_rank
        for head in range(2):
            cols = slice(head * HD, head * HD + HD)
            scores = lax.dot_general(
                qkv[0, rows, cols], qkv[1, :, cols], (((1,), (1,)), ((), ())), preferred_element_type=F32
            )
            scores = jnp.where(allowed, scores, -jnp.inf)
            peak = jnp.max(scores, axis=1, keepdims=True)
            expo = jnp.exp2((scores - peak) * EXP2_SCALE)
            total = jnp.sum(expo, axis=1, keepdims=True)
            mixed = jnp.dot(expo.astype(BF16), qkv[2, :, cols], preferred_element_type=F32)
            mixed = (mixed / total).astype(BF16)
            ctx_own[rows, cols] = mixed
            if rel == 0:
                ctx_all[128 * k : 128 * k + 128, pl.ds(mult(c * 1024 + x * 256 + head * HD, 128), HD)] = mixed
        for d in (1, -1):
            send(ctx_own.at[rows], ctx_spot(k, c, x), dev(0, 0, d, rel), "ctx", ("ctx", k, 1))
        if rel == 1:
            send(ctx_own.at[rows], ctx_spot(k, c, x), dev(0, 0, 0, 1), "ctx", ("ctx", k, 2))

    def ctx_pass(k):
        recv(ctx_all.at[:128, :1024], ("ctx", k, 1))
        for rel in range(2):
            for d in (1, -1):
                ref = ctx_spot(k, (c + rel) % 2, (x - d + X) % X, 0 if d == 1 else 1)
                send(ref, ref, dev(0, 0, d, 0), "ctx", ("ctx", k, 2))

    def ctx_end(k):
        recv(ctx_all.at[:128, :768], ("ctx", k, 2))

    for zz in range(Z):
        columns = pl.ds(mult(zz * 512 + x * 128, 128), 128)
        local(resid.at[:, c, :, columns], res.at[:, :, 128 * zz : 128 * zz + 128], "res")

    def stream_spot(k, cc, xx, half=None):
        row = (2 * k + cc) * 128
        rows = pl.ds(mult(row, 128), 128) if half is None else pl.ds(mult(row + half * 64, 64), 64)
        return stream.at[:, rows, pl.ds(mult(xx * 128, 128), 128)]

    def project(k):
        rows = pl.ds(mult((2 * k + c) * 128, 128), 128)
        columns = pl.ds(mult(x * 128, 128), 128)
        for block in range(4):
            part = jnp.dot(
                ctx_all[128 * k : 128 * k + 128, :], wo[:, 256 * block : 256 * block + 256], preferred_element_type=F32
            )
            part = part + res[k, :, 256 * block : 256 * block + 256].astype(F32)
            stream[2 * block, rows, columns] = part[:, :128].astype(BF16)
            stream[2 * block + 1, rows, columns] = part[:, 128:].astype(BF16)
        ref = stream_spot(k, c, x)
        for d in (1, -1):
            send(ref, ref, dev(0, 0, d, 0), "stream", ("stream", k, 1))
        send(ref, ref, dev(0, 0, 0, 1), "stream", ("across", k))

    def stream_pass(k, hop):
        recv(stream.at[:, : 256 // hop, :128], ("stream", k, hop))
        for d in (1, -1):
            half = 0 if d == 1 else 1
            if hop == 1:
                ref = stream_spot(k, c, (x - d + X) % X, half)
                send(ref, ref, dev(0, 0, d, 0), "stream", ("stream", k, 2))
            ref = stream_spot(k, c, (x - d * hop + X) % X, None if hop == 1 else half)
            send(ref, ref, dev(0, 0, 0, 1), "stream", ("across", k))

    def stream_end(k):
        recv(stream.at[:, :128, :], ("across", k))

    def norm_scale(k):
        rows = pl.ds(256 * k, 256)

        def add_squares(i, total):
            piece = stream[i, rows, :].astype(F32)
            piece = piece * piece
            return total + (piece[:, :128] + piece[:, 128:256]) + (piece[:, 256:384] + piece[:, 384:])

        squares = lax.fori_loop(0, Z, add_squares, jnp.zeros((256, 128), F32))
        total = jnp.sum(squares.T, axis=0, keepdims=True)
        scales[k] = lax.rsqrt(total * (1.0 / D) + 1e-5)

    def ff_part(k, *dzs):
        rows = slice(256 * k, 256 * k + 256)

        def one(half, _):
            at = pl.ds(mult(half * FF, 16), FF)
            total = None
            for dz in dzs:
                zz = (z + dz + Z) % Z
                part = lax.dot_general(
                    w[zz, at, :], stream[zz, rows, :], (((1,), (1,)), ((), ())), preferred_element_type=F32
                )
                total = part if total is None else total + part
            acc[at, rows] = total if 0 in dzs else acc[at, rows] + total
            return 0

        lax.fori_loop(0, 2, one, 0)

    def activate(k):
        rows = slice(256 * k, 256 * k + 256)
        scale = scales[k]
        for first in range(0, FF, 128):
            count = min(128, FF - first)
            gate = acc[first : first + count, rows] * scale
            up = acc[FF + first : FF + first + count, rows] * scale
            hid[first : first + count, rows] = (gate / (1.0 + jnp.exp(-gate)) * up).astype(BF16)
        local(hid.at[:, rows], hidden.at[:, rows], "hidden")

    y_event("A", 0, 1)
    share("v")
    share("q")
    z_start("A", -1)
    z_event("B", 0, 1)
    for unit in range(2):
        wo_y_wait(unit)
        wo_start(unit)
    y_start("B", 0)
    y_start("B", 1)
    y_start("B", -1)
    wo_event(0, 1)
    wo_event(1, 1)
    qkv_wait()
    attend(0, 1)
    attend(0, 0)
    wo_event(0, 2)
    attend(1, 1)
    attend(1, 0)
    wo_event(1, 2)
    z_wait("B", 0, 2)
    y_start("B", 2)
    y_start("B", -2)
    attend(2, 1)
    attend(2, 0)
    y_event("A", 0, 2)
    attend(3, 1)
    attend(3, 0)
    wo_event(0, 3)
    z_pass("B", 0, 2)
    ctx_pass(0)
    wo_event(1, 3)
    z_event("A", 0, 1)
    z_start("A", 1)
    ctx_pass(1)
    z_start("A", 2)
    y_event("B", 0, 1)
    wo_event(0, 4)
    wo_event(1, 4)
    ctx_pass(2)
    z_event("A", -1, 1)
    ctx_pass(3)
    local_wait(res, "res")
    wo_d_wait()
    ctx_end(0)
    project(0)
    y_event("B", -1, 1)
    y_event("B", 1, 1)
    ctx_end(1)
    project(1)
    z_event("B", 0, 3)
    y_start("B", 3)
    y_start("B", -3)
    y_event("B", 0, 2)
    stream_pass(0, 1)
    ctx_end(2)
    project(2)
    z_event("A", 0, 2)
    z_event("A", 1, 1)
    y_event("B", 2, 1)
    y_event("B", -2, 1)
    stream_pass(1, 1)
    ctx_end(3)
    project(3)
    z_event("A", 2, 1)
    z_event("A", -1, 2)
    z_event("B", 0, 4)
    y_start("B", 4)
    stream_pass(0, 2)
    y_event("B", -1, 2)
    y_event("B", 1, 2)
    stream_end(0)
    norm_scale(0)
    z_event("A", 0, 3)
    z_event("A", 1, 2)
    y_event("B", 3, 1)
    y_event("B", -3, 1)
    stream_pass(2, 1)
    ff_part(0, 0, 1, -1)
    z_event("A", 2, 2)
    z_event("A", -1, 3)
    stream_pass(1, 2)
    stream_end(1)
    norm_scale(1)
    ff_part(1, 0, 1, -1)
    y_event("B", 4, 1)
    stream_pass(3, 1)
    z_event("A", 1, 3)
    z_event("A", 2, 3)
    y_event("B", 2, 2)
    y_event("B", -2, 2)
    ff_part(0, 2, -2)
    stream_pass(2, 2)
    ff_part(1, 2, -2)
    stream_end(2)
    norm_scale(2)
    ff_part(2, 0, 1, -1)
    stream_pass(3, 2)
    ff_part(2, 2, -2)
    stream_end(3)
    norm_scale(3)
    for zz in range(Z):
        local(stream.at[zz, mine, :], resid_out.at[:, 512 * zz : 512 * zz + 512], "resid_out")
    ff_part(3, 0, 1, -1)
    ff_part(3, 2, -2)

    def early_sent():
        @pl.when(jnp.logical_not(collector))
        def _():
            sent(wo_in, "wo_x")

        @pl.when(collector)
        def _():
            sent(wo.at[:512, :512], "wo_y")

        @pl.when(ahead % 2 == 1)
        def _():
            sent(wo_block(0, 0, 0), "wo_y")

        sent(wo.at[:1024, :896], "wo_z")
        sent(wo.at[:1024, :], "wo_d")
        sent(qkv.at[:, :896], "qkv")
        sent(ctx_all.at[:448, :], "ctx")
        sent(stream.at[:, :896, :], "stream")
        sent(w_like("A", 3, 1), ("A", "y"))

    early_sent()
    y_event("B", 3, 2)
    y_event("B", -3, 2)
    for k in range(4):
        ff_part(k, 3, -3)
    for dy in (0, -1, 1, 2):
        z_event("A", dy, 4)
    y_event("B", 4, 2)
    for k in range(4):
        ff_part(k, 4)
        activate(k)
    sent(w_like("A", 7, 4), ("A", "z"))
    sent(w_like("B", 7, 1), ("B", "z"))
    sent(w_like("B", 6, 4), ("B", "y"))
    local_wait(stream.at[:4, :256, :], "resid_out")
    local_wait(hid, "hidden")
    assert (len(send_ids), len(recv_ids), len(local_ids)) == (N_SEND, N_RECV, N_LOCAL), (send_ids, recv_ids, local_ids)


def body(queries, keys, values, spans, resid_in, out_weight, norm_gain, gate_weight, up_weight):
    anywhere = pl.BlockSpec(memory_space=pl.ANY)
    resid_out, hidden = pl.pallas_call(
        kernel,
        out_shape=(jax.ShapeDtypeStruct((128, D), BF16), jax.ShapeDtypeStruct((FF, SEQ), BF16)),
        in_specs=[pl.BlockSpec(memory_space=pltpu.HBM)] * 9,
        out_specs=(anywhere, anywhere),
        scratch_shapes=[
            pltpu.VMEM((3, SEQ, 256), BF16),
            pltpu.VMEM((SEQ, 256), BF16),
            pltpu.VMEM((512, 2048), BF16),
            pltpu.VMEM((4, 128, 1024), BF16),
            pltpu.VMEM((Z, SEQ, 512), BF16),
            pltpu.VMEM((2048, 1024), BF16),
            pltpu.VMEM((Z, 2 * FF, 512), BF16),
            pltpu.VMEM((2 * FF, SEQ), F32),
            pltpu.VMEM((4, 1, 256), F32),
            pltpu.VMEM((FF, SEQ), BF16),
            pltpu.VMEM((1, 128), F32),
            pltpu.VMEM((FF, 128), BF16),
            pltpu.VMEM((FF, 128), BF16),
            pltpu.SMEM((1, 2), jnp.int32),
            pltpu.SemaphoreType.DMA((N_SEND,)),
            pltpu.SemaphoreType.DMA((N_RECV,)),
            pltpu.SemaphoreType.DMA((N_LOCAL,)),
        ],
        compiler_params=pltpu.CompilerParams(
            collective_id=0, has_side_effects=True, vmem_limit_bytes=VMEM_BYTES
        ),
    )(
        queries, keys, values, spans, resid_in.reshape(4, 2, 128, D), out_weight,
        norm_gain.reshape(D // 128, 128), gate_weight.T, up_weight.T,
    )
    return resid_out, hidden.T


def solution(mesh):
    return jax.shard_map(
        body,
        mesh=mesh,
        in_specs=(
            P(("dp", "ctx"), None),
            P(("dp", "ctx"), None),
            P(("dp", "ctx"), None),
            P("dp", None),
            P("dp", None),
            P("ctx", "dp"),
            P(),
            P("dp", "ctx"),
            P("dp", "ctx"),
        ),
        out_specs=(P(("dp", "ctx"), None), P("dp", "ctx")),
        check_vma=False,
    )
```

time: 138 us -> 114 us (0.83)
  Pallas kernels: 134 us -> 110 us
    pallas_call x1, Pallas kernels: 134 us -> 110 us  [body(): pl.pallas_call(kernel, out_shape=(jax.ShapeDtypeStruct((128, D), BF16), j...]
where the time goes in v3:
time: 114 us
  Pallas kernels  110 us (96%)
  local copies, waits for them, and re-layouts  3.49 us (3%)
    pallas_call x1, Pallas kernels, body(): pl.pallas_call(kernel, out_shape=(jax.ShapeDtypeStruct((128, D), BF16), j...  110 us
    unnamed x4, local copies, waits for them, and re-layouts  3.49 us

profile of v3, /device:TPU:9, one launch (start us, length us, event | category | flops | bytes accessed | tf_op | source)
XLA Modules:
  0.0 113.7 jit_solution(782013685849563814)
XLA Ops:
  0.6 109.6 %shard_map.104 = (bf16[128,4096]{1,0:T(8,128)(2,1)}, bf16[688,1024]{1,0:T(8,128)(2,1)}) custom-call(bf16[128,2048]{1,0:T(8,128)(2,1)} %q_in.1, bf16[128,2048]{1,0:T(8,128)(2,1)} %k_in.1, bf16[128,2048]{1,0:T(8,128)(2,1)} %v_in.1, s32[1,2]{1,0:T(1,128)} %spans_in.1, bf16[4,2,128,4096]{3,2,1,0:T(8,128)(2,1)} %bitcast.5, bf16[256,128]{1,0:T(8,128)(2,1)} %wo_in.1, ...), custom_call_target="tpu_custom_call" | custom-call | tf_op jit(solution)/shard_map/pallas_call | solution.py:485
  110.2 0.0 copy-start
  110.2 2.4 %copy.13 = bf16[128,4096]{1,0:T(8,128)(2,1)} copy(bf16[128,4096]{1,0:T(8,128)(2,1)} %get-tuple-element.8) | data formatting | bytes 2097152
  112.6 0.0 copy-done
  112.6 1.1 copy.14
Async XLA Ops:
  110.2 2.4 %copy-start = (bf16[688,1024]{1,0:T(8,128)(2,1)S(1)}, bf16[688,1024]{1,0:T(8,128)(2,1)}, u32[]{:S(2)}) copy-start(bf16[688,1024]{1,0:T(8,128)(2,1)} %get-tuple-element.5) | copy-start | bytes 4227076

commit v4 on v3

--- a/solution.py
+++ b/solution.py
@@ -12,7 +12,7 @@
 Z, Y, X = 8, 4, 4
 HD = 128
 SEQ, D, FF = 1024, 4096, 688
-PART_ROWS = {"A": (0, 512), "B": (512, 2 * FF - 512)}
+PART_ROWS = {"A": (0, 448), "B": (448, 2 * FF - 448)}
 EXP2_SCALE = math.log2(math.e) / math.sqrt(HD)
 F32, BF16 = jnp.float32, jnp.bfloat16
 VMEM_BYTES = 56 * 1024 * 1024
@@ -72,7 +72,6 @@
     peers += [(0, 1, 0, 0), (0, 2, 0, 0), (0, 3, 0, 0), (1, 0, 0, 0), (-1, 0, 0, 0)]
     for peer in peers:
         pl.semaphore_signal(barrier, inc=1, device_id=dev(*peer), device_id_type=MESH)
-    pl.semaphore_wait(barrier, len(peers))
 
     def wo_block(zz, cc, unit=None):
         rows = pl.ds(mult(cc * 1024, 1024), 1024) if unit is None else pl.ds(mult(cc * 1024 + unit * 512, 512), 512)
@@ -83,10 +82,6 @@
 
     ahead = (y - x + X) % X
     collector = ahead == 0
-
-    @pl.when(jnp.logical_not(collector))
-    def _():
-        send(wo_in, wo_rows(x), dev(0, 0, ahead, 0), "wo_x", "wo_x")
 
     def pack_own():
         local_wait(gate_in, "gate")
@@ -98,6 +93,14 @@
         w[z, FF:, columns] = (up_in[...].astype(F32) * gain_row).astype(BF16)
 
     pack_own()
+    pl.semaphore_wait(barrier, len(peers))
+
+    @pl.when(jnp.logical_not(collector))
+    def _():
+        for piece in range(4):
+            rows = pl.ds(mult(c * 1024 + x * 256 + piece * 64, 64), 64)
+            target = wo.at[rows, pl.ds(mult(z * 128, 128), 128)]
+            send(wo_in.at[64 * piece : 64 * piece + 64, :], target, dev(0, 0, ahead, 0), "wo_x", "wo_x")
 
     def w_block(part, dz, dy, half=None):
         first, count = PART_ROWS[part]
@@ -147,6 +150,10 @@
     y_start("A", 0)
     z_start("B", 0)
     z_start("A", 0)
+
+    @pl.when(jnp.logical_not(collector))
+    def _():
+        y_start("B", 0)
 
     mine = pl.ds(mult(cx * 128, 128), 128)
     shares = {"k": (1, k_in), "v": (2, v_in), "q": (0, q_in)}
@@ -161,16 +168,18 @@
 
     share("k")
 
+    def wo_along_y(unit, d):
+        ref = wo_block(z, c, unit)
+        send(ref, ref, dev(0, d, 0, 0), "wo_y", ("wo_y", unit))
+
     @pl.when(collector)
     def _():
         recv(wo.at[:256, :384], "wo_x")
         own_part = pltpu.make_async_copy(wo_in, wo_rows(x), local_sem.at[local_ids.setdefault("wo", len(local_ids))])
         own_part.start()
         own_part.wait()
-        for unit in range(2):
-            for d in (1, -1):
-                ref = wo_block(z, c, unit)
-                send(ref, ref, dev(0, d, 0, 0), "wo_y", ("wo_y", unit))
+        wo_along_y(0, 1)
+        wo_along_y(1, -1)
 
     def wo_y_wait(unit):
         @pl.when(jnp.logical_not(collector))
@@ -181,8 +190,7 @@
 
         @pl.when(ahead == d % Y)
         def _():
-            ref = wo_block(z, c, unit)
-            send(ref, ref, dev(0, d, 0, 0), "wo_y", ("wo_y", unit))
+            wo_along_y(unit, d)
 
     def wo_across(dz, unit):
         ref = wo_block(z + dz, c, unit)
@@ -333,113 +341,164 @@
             gate = acc[first : first + count, rows] * scale
             up = acc[FF + first : FF + first + count, rows] * scale
             hid[first : first + count, rows] = (gate / (1.0 + jnp.exp(-gate)) * up).astype(BF16)
-        local(hid.at[:, rows], hidden.at[:, rows], "hidden")
+            if first in (256, 640):
+                done = slice(0, 384) if first == 256 else slice(384, FF)
+                local(hid.at[done, rows], hidden.at[done, rows], "hidden")
 
     y_event("A", 0, 1)
     share("v")
     share("q")
-    z_start("A", -1)
-    z_event("B", 0, 1)
-    for unit in range(2):
-        wo_y_wait(unit)
-        wo_start(unit)
-    y_start("B", 0)
-    y_start("B", 1)
-    y_start("B", -1)
-    wo_event(0, 1)
-    wo_event(1, 1)
+
+    def fill_z():
+        z_start("A", -1)
+        z_pass("B", 0, 1)
+
+    z_wait("B", 0, 1)
+
+    @pl.when(collector)
+    def _():
+        wo_along_y(1, 1)
+        wo_along_y(0, -1)
+
+    @pl.when(jnp.logical_not(collector))
+    def _():
+        fill_z()
+
+    def next_y():
+        y_start("B", 1)
+        y_start("B", -1)
+
+    @pl.when(ahead == 2)
+    def _():
+        next_y()
+
+    def wo_units(*units):
+        for unit in units:
+            wo_y_wait(unit)
+            wo_start(unit)
+
+    @pl.when(ahead == 3)
+    def _():
+        wo_units(1, 0)
+
+    @pl.when(ahead != 3)
+    def _():
+        wo_units(0, 1)
+
+    @pl.when(collector)
+    def _():
+        y_start("B", 0)
+        wo_event(0, 1)
+        wo_event(1, 1)
+        fill_z()
+
+    @pl.when(ahead != 2)
+    def _():
+        next_y()
+
     qkv_wait()
     attend(0, 1)
     attend(0, 0)
-    wo_event(0, 2)
+
+    @pl.when(jnp.logical_not(collector))
+    def _():
+        wo_event(0, 1)
+
     attend(1, 1)
     attend(1, 0)
+
+    @pl.when(jnp.logical_not(collector))
+    def _():
+        wo_event(1, 1)
+
+    y_event("B", 0, 1)
+    attend(2, 1)
+    attend(2, 0)
+    wo_event(0, 2)
+    attend(3, 1)
+    attend(3, 0)
     wo_event(1, 2)
     z_wait("B", 0, 2)
     y_start("B", 2)
     y_start("B", -2)
-    attend(2, 1)
-    attend(2, 0)
+    ctx_pass(0)
+    wo_event(0, 3)
+    ctx_pass(1)
     y_event("A", 0, 2)
-    attend(3, 1)
-    attend(3, 0)
-    wo_event(0, 3)
+    wo_event(1, 3)
     z_pass("B", 0, 2)
-    ctx_pass(0)
-    wo_event(1, 3)
+    ctx_pass(2)
+    y_event("B", -1, 1)
+    y_event("B", 1, 1)
+    wo_event(0, 4)
+    wo_event(1, 4)
     z_event("A", 0, 1)
     z_start("A", 1)
-    ctx_pass(1)
     z_start("A", 2)
-    y_event("B", 0, 1)
-    wo_event(0, 4)
-    wo_event(1, 4)
-    ctx_pass(2)
-    z_event("A", -1, 1)
     ctx_pass(3)
     local_wait(res, "res")
     wo_d_wait()
     ctx_end(0)
     project(0)
-    y_event("B", -1, 1)
-    y_event("B", 1, 1)
+    z_event("A", -1, 1)
     ctx_end(1)
     project(1)
     z_event("B", 0, 3)
     y_start("B", 3)
     y_start("B", -3)
-    y_event("B", 0, 2)
     stream_pass(0, 1)
     ctx_end(2)
     project(2)
+    y_event("B", 2, 1)
+    y_event("B", -2, 1)
     z_event("A", 0, 2)
     z_event("A", 1, 1)
-    y_event("B", 2, 1)
-    y_event("B", -2, 1)
+    z_event("A", 2, 1)
+    z_event("A", -1, 2)
     stream_pass(1, 1)
     ctx_end(3)
     project(3)
-    z_event("A", 2, 1)
-    z_event("A", -1, 2)
     z_event("B", 0, 4)
     y_start("B", 4)
     stream_pass(0, 2)
+    stream_end(0)
+    norm_scale(0)
+    y_event("B", 0, 2)
     y_event("B", -1, 2)
     y_event("B", 1, 2)
-    stream_end(0)
-    norm_scale(0)
+    ff_part(0, 0, 1, -1)
+    stream_pass(2, 1)
+    y_event("B", 3, 1)
+    y_event("B", -3, 1)
+    stream_pass(1, 2)
     z_event("A", 0, 3)
     z_event("A", 1, 2)
-    y_event("B", 3, 1)
-    y_event("B", -3, 1)
-    stream_pass(2, 1)
-    ff_part(0, 0, 1, -1)
     z_event("A", 2, 2)
     z_event("A", -1, 3)
-    stream_pass(1, 2)
     stream_end(1)
     norm_scale(1)
     ff_part(1, 0, 1, -1)
+    stream_pass(3, 1)
     y_event("B", 4, 1)
-    stream_pass(3, 1)
-    z_event("A", 1, 3)
-    z_event("A", 2, 3)
     y_event("B", 2, 2)
     y_event("B", -2, 2)
     ff_part(0, 2, -2)
+    z_event("A", 1, 3)
+    ff_part(1, 2, -2)
     stream_pass(2, 2)
-    ff_part(1, 2, -2)
+    z_event("A", 2, 3)
+    y_event("B", 3, 2)
+    y_event("B", -3, 2)
+    ff_part(0, 3, -3)
+    stream_pass(3, 2)
+    ff_part(1, 3, -3)
     stream_end(2)
     norm_scale(2)
-    ff_part(2, 0, 1, -1)
-    stream_pass(3, 2)
-    ff_part(2, 2, -2)
+    ff_part(2, 0, 1, -1, 2, -2, 3, -3)
     stream_end(3)
-    norm_scale(3)
     for zz in range(Z):
         local(stream.at[zz, mine, :], resid_out.at[:, 512 * zz : 512 * zz + 512], "resid_out")
-    ff_part(3, 0, 1, -1)
-    ff_part(3, 2, -2)
+    norm_scale(3)
 
     def early_sent():
         @pl.when(jnp.logical_not(collector))
@@ -462,16 +521,14 @@
         sent(w_like("A", 3, 1), ("A", "y"))
 
     early_sent()
-    y_event("B", 3, 2)
-    y_event("B", -3, 2)
-    for k in range(4):
-        ff_part(k, 3, -3)
     for dy in (0, -1, 1, 2):
         z_event("A", dy, 4)
     y_event("B", 4, 2)
-    for k in range(4):
+    for k in range(3):
         ff_part(k, 4)
         activate(k)
+    ff_part(3, 0, 1, -1, 2, -2, 3, -3, 4)
+    activate(3)
     sent(w_like("A", 7, 4), ("A", "z"))
     sent(w_like("B", 7, 1), ("B", "z"))
     sent(w_like("B", 6, 4), ("B", "y"))

time: 114 us -> 108 us (0.947)
  Pallas kernels: 110 us -> 104 us
    pallas_call x1, Pallas kernels: 110 us -> 104 us  [body(): pl.pallas_call(kernel, out_shape=(jax.ShapeDtypeStruct((128, D), BF16), j...]
where the time goes in v4:
time: 108 us
  Pallas kernels  104 us (96%)
  local copies, waits for them, and re-layouts  3.49 us (3%)
    pallas_call x1, Pallas kernels, body(): pl.pallas_call(kernel, out_shape=(jax.ShapeDtypeStruct((128, D), BF16), j...  104 us
    unnamed x4, local copies, waits for them, and re-layouts  3.49 us

profile of v4, /device:TPU:9, one launch (start us, length us, event | category | flops | bytes accessed | tf_op | source)
XLA Modules:
  0.0 108.3 jit_solution(17343530788174194136)
XLA Ops:
  0.6 104.1 %shard_map.104 = (bf16[128,4096]{1,0:T(8,128)(2,1)}, bf16[688,1024]{1,0:T(8,128)(2,1)}) custom-call(bf16[128,2048]{1,0:T(8,128)(2,1)} %q_in.1, bf16[128,2048]{1,0:T(8,128)(2,1)} %k_in.1, bf16[128,2048]{1,0:T(8,128)(2,1)} %v_in.1, s32[1,2]{1,0:T(1,128)} %spans_in.1, bf16[4,2,128,4096]{3,2,1,0:T(8,128)(2,1)} %bitcast.5, bf16[256,128]{1,0:T(8,128)(2,1)} %wo_in.1, ...), custom_call_target="tpu_custom_call" | custom-call | tf_op jit(solution)/shard_map/pallas_call | solution.py:542
  104.8 0.0 copy-start
  104.8 2.4 %copy.13 = bf16[128,4096]{1,0:T(8,128)(2,1)} copy(bf16[128,4096]{1,0:T(8,128)(2,1)} %get-tuple-element.8) | data formatting | bytes 2097152
  107.2 0.0 copy-done
  107.2 1.1 %copy.14 = bf16[1024,688]{0,1:T(8,128)(2,1)} copy(bf16[1024,688]{0,1:T(8,128)(2,1)S(1)} %bitcast.6) | data formatting | bytes 2818048
Async XLA Ops:
  104.8 2.4 %copy-start = (bf16[688,1024]{1,0:T(8,128)(2,1)S(1)}, bf16[688,1024]{1,0:T(8,128)(2,1)}, u32[]{:S(2)}) copy-start(bf16[688,1024]{1,0:T(8,128)(2,1)} %get-tuple-element.5) | copy-start | bytes 4227076

commit v5 on v4

--- a/solution.py
+++ b/solution.py
@@ -16,7 +16,7 @@
 EXP2_SCALE = math.log2(math.e) / math.sqrt(HD)
 F32, BF16 = jnp.float32, jnp.bfloat16
 VMEM_BYTES = 56 * 1024 * 1024
-N_SEND, N_RECV, N_LOCAL = 11, 73, 9
+N_SEND, N_RECV, N_LOCAL = 11, 74, 9
 
 
 def mult(value, of):
@@ -62,6 +62,20 @@
     def local_wait(as_large, kind):
         pltpu.make_async_copy(as_large, as_large, local_sem.at[local_ids[kind]]).wait()
 
+    def wo_block(zz, cc, unit=None):
+        rows = pl.ds(mult(cc * 1024, 1024), 1024) if unit is None else pl.ds(mult(cc * 1024 + unit * 512, 512), 512)
+        return wo.at[rows, pl.ds(mult((zz + Z) % Z * 128, 128), 128)]
+
+    def wo_rows(xx):
+        return wo.at[pl.ds(mult(c * 1024 + xx * 256, 256), 256), pl.ds(mult(z * 128, 128), 128)]
+
+    ahead = (y - x + X) % X
+    collector = ahead == 0
+
+    @pl.when(collector)
+    def _():
+        local(wo_in, wo_rows(x), "wo")
+
     local(gate_hbm, gate_in, "gate")
     local(up_hbm, up_in, "up")
     local(gain_in.at[pl.ds(dp, 1), :], gain, "gain")
@@ -73,15 +87,6 @@
     for peer in peers:
         pl.semaphore_signal(barrier, inc=1, device_id=dev(*peer), device_id_type=MESH)
 
-    def wo_block(zz, cc, unit=None):
-        rows = pl.ds(mult(cc * 1024, 1024), 1024) if unit is None else pl.ds(mult(cc * 1024 + unit * 512, 512), 512)
-        return wo.at[rows, pl.ds(mult((zz + Z) % Z * 128, 128), 128)]
-
-    def wo_rows(xx):
-        return wo.at[pl.ds(mult(c * 1024 + xx * 256, 256), 256), pl.ds(mult(z * 128, 128), 128)]
-
-    ahead = (y - x + X) % X
-    collector = ahead == 0
 
     def pack_own():
         local_wait(gate_in, "gate")
@@ -160,10 +165,13 @@
 
     def share(name):
         which, source = shares[name]
-        for dx, dc in [(2, 0), (2, 1), (1, 0), (1, 1), (3, 0), (3, 1), (0, 1)]:
+        for dx, dc in [(0, 1), (2, 0), (2, 1), (1, 0), (1, 1), (3, 0), (3, 1)]:
             target = dev(0, 0, dx, dc)
             columns = pl.ds(mult(target[1] * 256, 256), 256)
-            send(source.at[:, columns], qkv.at[which, mine], target, "qkv", name)
+            event = "sibling" if dx == 0 and name == "k" else name
+            send(source.at[:, columns], qkv.at[which, mine], target, "qkv", event)
+            if event == "sibling":
+                recv(qkv.at[0, :128], event)
         local(source.at[:, pl.ds(mult(cx * 256, 256), 256)], qkv.at[which, mine], "qkv")
 
     share("k")
@@ -175,9 +183,7 @@
     @pl.when(collector)
     def _():
         recv(wo.at[:256, :384], "wo_x")
-        own_part = pltpu.make_async_copy(wo_in, wo_rows(x), local_sem.at[local_ids.setdefault("wo", len(local_ids))])
-        own_part.start()
-        own_part.wait()
+        local_wait(wo_rows(x), "wo")
         wo_along_y(0, 1)
         wo_along_y(1, -1)
 
@@ -218,7 +224,7 @@
     def qkv_wait():
         local_wait(qkv.at[:, :128, :], "qkv")
         for name in shares:
-            recv(qkv.at[0, :896], name)
+            recv(qkv.at[0, : 768 if name == "k" else 896], name)
 
     local_wait(spans, "spans")
     prefix_end, middle_end = spans[0, 0], spans[0, 1]
@@ -387,16 +393,21 @@
 
     @pl.when(collector)
     def _():
+        wo_event(0, 1)
         y_start("B", 0)
-        wo_event(0, 1)
         wo_event(1, 1)
         fill_z()
 
-    @pl.when(ahead != 2)
+    @pl.when(collector)
     def _():
         next_y()
 
     qkv_wait()
+
+    @pl.when(ahead % 2 == 1)
+    def _():
+        next_y()
+
     attend(0, 1)
     attend(0, 0)
 
@@ -426,11 +437,11 @@
     ctx_pass(1)
     y_event("A", 0, 2)
     wo_event(1, 3)
-    z_pass("B", 0, 2)
     ctx_pass(2)
     y_event("B", -1, 1)
     y_event("B", 1, 1)
     wo_event(0, 4)
+    z_pass("B", 0, 2)
     wo_event(1, 4)
     z_event("A", 0, 1)
     z_start("A", 1)
@@ -475,14 +486,14 @@
     z_event("A", 1, 2)
     z_event("A", 2, 2)
     z_event("A", -1, 3)
+    y_event("B", 2, 2)
+    y_event("B", -2, 2)
+    ff_part(0, 2, -2)
     stream_end(1)
     norm_scale(1)
     ff_part(1, 0, 1, -1)
     stream_pass(3, 1)
     y_event("B", 4, 1)
-    y_event("B", 2, 2)
-    y_event("B", -2, 2)
-    ff_part(0, 2, -2)
     z_event("A", 1, 3)
     ff_part(1, 2, -2)
     stream_pass(2, 2)
@@ -494,7 +505,6 @@
     ff_part(1, 3, -3)
     stream_end(2)
     norm_scale(2)
-    ff_part(2, 0, 1, -1, 2, -2, 3, -3)
     stream_end(3)
     for zz in range(Z):
         local(stream.at[zz, mine, :], resid_out.at[:, 512 * zz : 512 * zz + 512], "resid_out")
@@ -524,7 +534,9 @@
     for dy in (0, -1, 1, 2):
         z_event("A", dy, 4)
     y_event("B", 4, 2)
-    for k in range(3):
+    ff_part(2, 0, 1, -1, 2, -2, 3, -3, 4)
+    activate(2)
+    for k in range(2):
         ff_part(k, 4)
         activate(k)
     ff_part(3, 0, 1, -1, 2, -2, 3, -3, 4)

time: 108 us -> 106 us (0.981)
  Pallas kernels: 104 us -> 101 us
    pallas_call x1, Pallas kernels: 104 us -> 101 us  [body(): pl.pallas_call(kernel, out_shape=(jax.ShapeDtypeStruct((128, D), BF16), j...]
where the time goes in v5:
time: 106 us; the launch traced here: 105 us
  Pallas kernels  101 us (95%)
  local copies, waits for them, and re-layouts  3.49 us (3%)
    pallas_call x1, Pallas kernels, body(): pl.pallas_call(kernel, out_shape=(jax.ShapeDtypeStruct((128, D), BF16), j...  101 us
    unnamed x4, local copies, waits for them, and re-layouts  3.49 us

profile of v5, /device:TPU:9, one launch (start us, length us, event | category | flops | bytes accessed | tf_op | source)
XLA Modules:
  0.0 105.4 jit_solution(13007687385445639942)
XLA Ops:
  0.6 101.2 %shard_map.104 = (bf16[128,4096]{1,0:T(8,128)(2,1)}, bf16[688,1024]{1,0:T(8,128)(2,1)}) custom-call(bf16[128,2048]{1,0:T(8,128)(2,1)} %q_in.1, bf16[128,2048]{1,0:T(8,128)(2,1)} %k_in.1, bf16[128,2048]{1,0:T(8,128)(2,1)} %v_in.1, s32[1,2]{1,0:T(1,128)} %spans_in.1, bf16[4,2,128,4096]{3,2,1,0:T(8,128)(2,1)} %bitcast.5, bf16[256,128]{1,0:T(8,128)(2,1)} %wo_in.1, ...), custom_call_target="tpu_custom_call" | custom-call | tf_op jit(solution)/shard_map/pallas_call | solution.py:554
  101.9 0.0 copy-start
  101.9 2.4 %copy.13 = bf16[128,4096]{1,0:T(8,128)(2,1)} copy(bf16[128,4096]{1,0:T(8,128)(2,1)} %get-tuple-element.8) | data formatting | bytes 2097152
  104.3 0.0 copy-done
  104.3 1.1 %copy.14 = bf16[1024,688]{0,1:T(8,128)(2,1)} copy(bf16[1024,688]{0,1:T(8,128)(2,1)S(1)} %bitcast.6) | data formatting | bytes 2818048
Async XLA Ops:
  101.9 2.4 %copy-start = (bf16[688,1024]{1,0:T(8,128)(2,1)S(1)}, bf16[688,1024]{1,0:T(8,128)(2,1)}, u32[]{:S(2)}) copy-start(bf16[688,1024]{1,0:T(8,128)(2,1)} %get-tuple-element.5) | copy-start | bytes 4227076
